TPU v7x, 256 devices: a whole 4x4x8 slice. The times are simulated.
256 devices in a mesh: outer: 8 (over z_hi, y), inner: 32 (over z_lo, x, core).
Axes of the slice: x: 4, y: 4, z: 8 (z_hi: 2, z_lo: 4; z = z_hi * 4 + z_lo), core: 2. Of those that a mesh axis runs over, the one named last changes fastest.
Arguments:
- inputs: bfloat16 [4096, 6144], P('outer'), may hold values from -6 to 6
- act_grad: bfloat16 [4096, 24576], P('outer', 'inner'), may hold values from -6 to 6
- in_codes: bfloat16 [6144, 24576], P('outer', 'inner'), may hold values from -6 to 6
- in_scales: bfloat16 [6144], P('outer'), may hold values from 0.0038146973 to 0.038085938
Outputs:
- input_grad: bfloat16 [4096, 6144], P(('outer', 'inner'))
- in_grad: float32 [6144, 24576], P('outer', 'inner')
All inputs are finite; a program needn't handle non-finite values.
Results may differ from a plain program's by a relative error of at most 0.0065.
Values may be sent and summed in bfloat16 or wider, within the bound.
A program may use at most 128 MiB of HBM per device.

v0:
```python
import jax
import jax.numpy as jnp
from jax import lax
from jax.sharding import PartitionSpec as P

coef = 0.7978845608
cubic = 0.044715


def gelu_slope(value):
    tangent = jnp.tanh(coef * (value + cubic * value * value * value))
    return 0.5 * (1.0 + tangent) + 0.5 * value * (1.0 - tangent * tangent) * coef * (
        1.0 + 3.0 * cubic * value * value
    )


def dequant(codes, scales):
    return (codes.astype(jnp.float32) * scales.astype(jnp.float32)[:, None]).astype(jnp.bfloat16)


def local(inputs, act_grad, in_codes, in_scales):
    n_outer = lax.axis_size("outer")
    codes, scales = (
        lax.all_gather(in_codes, "outer", axis=0, tiled=True),
        lax.all_gather(in_scales, "outer", axis=0, tiled=True),
    )
    w_in = dequant(codes, scales)
    hidden = jnp.dot(inputs, w_in, preferred_element_type=jnp.float32)
    hid_grad = (act_grad.astype(jnp.float32) * gelu_slope(hidden)).astype(jnp.bfloat16)
    input_grad = lax.psum_scatter(
        lax.dot_general(
            hid_grad, w_in, (((1,), (1,)), ((), ())), preferred_element_type=jnp.float32
        ),
        "inner",
        scatter_dimension=0,
        tiled=True,
    ).astype(jnp.bfloat16)
    term = lax.dot_general(
        inputs, hid_grad, (((0,), (0,)), ((), ())), preferred_element_type=jnp.float32
    )
    in_grad = lax.psum_scatter(term, "outer", scatter_dimension=0, tiled=True) / n_outer
    return (input_grad, in_grad)


def solution(mesh):
    return jax.shard_map(
        local,
        mesh=mesh,
        in_specs=(P("outer", None), P("outer", "inner"), P("outer", "inner"), P("outer")),
        out_specs=(P(("outer", "inner"), None), P("outer", "inner")),
        check_vma=False,
    )
```

profile of v0, /device:TPU:32, one launch (start us, length us, event | category | flops | bytes accessed | tf_op | source)
XLA Modules:
  0.0 738.7 jit_solution(12380545437643937980)
XLA Ops:
  7.2 0.0 all-gather.3.cloned.1.call-start
  7.2 0.7 all-gather.3.cloned.1.call-update
  7.9 0.0 reduce-scatter.3.cloned.1.call-start
  7.9 0.7 reshape.5
  8.6 48.5 %all-gather = bf16[8,1,768]{2,1,0:T(2,128)(2,1)S(1)} all-gather(bf16[1,1,768]{2,1,0:T(2,128)(2,1)S(1)} %reshape.5), channel_id=1, replica_groups=mesh['outer'=8,'inner'=32] {'outer'}, dimensions={0}, use_global_device_ids=true | all-gather | bytes 13824 | tf_op jit(solution)/shard_map/all_gather | solution.py:25
  57.2 1.4 copy.8
  58.6 143.5 %all-gather.3.cloned.1.call-done = bf16[6144,768]{1,0:T(8,128)(2,1)} async-done(((bf16[768,768]{1,0:T(8,128)(2,1)}), bf16[6144,768]{1,0:T(8,128)(2,1)}) %all-gather.3.cloned.1.call-update) | async-done | bytes 9437200 | tf_op jit(solution)/shard_map/all_gather | solution.py:24
  202.1 0.0 copy-start
  202.1 12.5 %fusion.8 = bf16[512,768]{0,1:T(8,128)(2,1)S(1)} fusion(bf16[512,6144]{1,0:T(8,128)(2,1)} %param.4, bf16[6144,768]{1,0:T(8,128)(2,1)} %all-gather.3.cloned.1.call-done, f32[6144]{0:T(1024)S(1)} %bitcast.19, bf16[512,768]{0,1:T(8,128)(2,1)S(1)} %copy.8), kind=kOutput, calls=%fused_computation.12 | convolution fusion | flops 4853858304 | bytes 17326080 | tf_op jit(solution)/shard_map/dot_general | solution.py:28
  214.6 0.0 copy-done
  214.6 9.0 %fusion = f32[512,6144]{1,0:T(8,128)} fusion(bf16[512,768]{0,1:T(8,128)(2,1)S(1)} %fusion.8, bf16[6144,768]{1,0:T(8,128)(2,1)S(1)} %copy-done, f32[6144]{0:T(1024)S(1)} %bitcast.20), kind=kOutput, calls=%fused_computation.2 | convolution fusion | flops 4845993984 | bytes 22831104 | tf_op jit(solution)/shard_map/dot_general | solution.py:31
  223.6 0.0 reduce-scatter.3.cloned.1.call-update
  223.7 0.2 reduce-scatter.5.cloned.1.call-start
  223.9 11.9 %convolution_bitcast_fusion = f32[6144,768]{0,1:T(8,128)} fusion(bf16[512,768]{0,1:T(8,128)(2,1)S(1)} %fusion.8, bf16[512,6144]{1,0:T(8,128)(2,1)} %param.4), kind=kOutput, calls=%fused_computation.1 | convolution fusion | flops 4831838208 | bytes 25952256 | tf_op jit(solution)/shard_map/dot_general | solution.py:38
  235.8 0.0 reduce-scatter.5.cloned.1.call-update
  235.8 127.5 %reduce-scatter.3.cloned.1.call-done = f32[16,6144]{1,0:T(8,128)} async-done(((f32[512,6144]{1,0:T(8,128)}), f32[16,6144]{1,0:T(8,128)}) %reduce-scatter.3.cloned.1.call-update) | async-done | bytes 393232 | tf_op jit(solution)/shard_map/reduce_scatter | solution.py:30
  363.3 1.7 convert_element_type.23
  365.0 363.5 %reduce-scatter.5.cloned.1.call-done = f32[768,768]{0,1:T(8,128)} async-done(((f32[6144,768]{0,1:T(8,128)}), f32[768,768]{0,1:T(8,128)}) %reduce-scatter.5.cloned.1.call-update) | async-done | bytes 2359312 | tf_op jit(solution)/shard_map/reduce_scatter | solution.py:41
  728.4 1.8 broadcast_multiply_fusion
  730.2 2.0 copy.9
  (1 shorter events, 0.0 us)
Async XLA Ops:
  7.2 194.9 %all-gather.3.cloned.1.call-start = ((), (), s32[]{:S(2)}) async-start(), calls=%async_computation.2 | async-start | bytes 10616832 | tf_op jit(solution)/shard_map/all_gather | solution.py:24
  7.9 355.4 %reduce-scatter.3.cloned.1.call-start = ((), (), s32[]{:S(2)}) async-start(), calls=%async_computation.3 | async-start | bytes 12976128 | tf_op jit(solution)/shard_map/reduce_scatter | solution.py:30
  202.1 12.5 %copy-start = (bf16[6144,768]{1,0:T(8,128)(2,1)S(1)}, bf16[6144,768]{1,0:T(8,128)(2,1)}, u32[]{:S(2)}) copy-start(bf16[6144,768]{1,0:T(8,128)(2,1)} %all-gather.3.cloned.1.call-done) | copy-start | bytes 28311556
  223.7 504.8 %reduce-scatter.5.cloned.1.call-start = ((), (), s32[]{:S(2)}) async-start(), calls=%async_computation.4 | async-start | bytes 21233664 | tf_op jit(solution)/shard_map/reduce_scatter | solution.py:41
Sparse Core Ops, SparseCore 0:
  10.6 191.4 all-gather.2
  223.8 139.4 reduce-scatter.2
  367.6 360.8 reduce-scatter.4
where the time goes:
time: 739 us
  waiting for transfers between devices  635 us (86%)
  blocking collectives  48.5 us (7%)
  matrix products  33.4 us (5%)
  between operations  13.8 us (2%)
    reduce_scatter x1, waiting for transfers between devices, local(): lax.psum_scatter(term, 'outer', scatter_dimension=0, tiled=True) / n_outer  363 us
    all_gather x1, waiting for transfers between devices, local(): lax.all_gather(in_codes, 'outer', axis=0, tiled=True)  143 us
    reduce_scatter x1, waiting for transfers between devices, local(): lax.psum_scatter(lax.dot_general(hid_grad, w_in, (((1,), (1,)), ((), ()))...  127 us
    all_gather x1, blocking collectives, local(): lax.all_gather(in_scales, 'outer', axis=0, tiled=True)  48.5 us
  transfers between devices with their start and end apart: 3, of which 3 were waited for; matrix products, arithmetic and copies ran while one was open for 2% of the time, Pallas kernels for 0%

commit v1 on v0

v1 whole, which is shorter than its diff:
```python
import functools

import jax
import jax.numpy as jnp
from jax import lax
from jax.experimental import pallas as pl
from jax.experimental.pallas import tpu as pltpu
from jax.sharding import PartitionSpec as P

coef = 0.7978845608
cubic = 0.044715

MESH = pl.DeviceIdType.MESH
F32 = jnp.float32
BF16 = jnp.bfloat16

F = 3
T = 4
K = F * T
FC = 256
TC = 128
DB = 768
DP = 1536
COLS = 256

O_X1, O_X2, O_S3, O_S4, O_S5, O_S6, O_S7, O_S8, O_R1, O_R2, O_R3 = 0, 1, 2, 3, 5, 7, 8, 10, 9, 10, 11
STEPS = K + O_R3


def gelu_slope(value):
    tangent = jnp.tanh(coef * (value + cubic * value * value * value))
    return 0.5 * (1.0 + tangent) + 0.5 * value * (1.0 - tangent * tangent) * coef * (
        1.0 + 3.0 * cubic * value * value
    )


def kernel(
    x_hbm, act_hbm, w_hbm, ig_ref, gw_hbm,
    xs, ws, act, send_b, recv_b, keep, send_z, recv_z, hg, term,
    acc, send_c, recv_c, send_x, recv_x, keep_x, send_l, recv_l, keep_l,
    send_f, fin, send_a, recv_a, gout,
    sem_own, sem_wo, sem_act, sem_gw,
    xb_s, xb_r, xz_s, xz_r, xd_s, xd_r, xx_s, xx_r, xc_s, xc_r, xe_s, xe_r,
    w_s, w_r, b_s, b_r, z_s, z_r, gz_s, gz_r, g0_s, g0_r, g1_s, g1_r,
    a_s, a_r, c_s, c_r, rx_s, rx_r, l_s, l_r, f_s, f_r,
):
    o = lax.axis_index("outer")
    i = lax.axis_index("inner")
    h, y = o // 4, o % 4
    l, x, c = i // 8, (i // 2) % 4, i % 2
    pair, side = y // 2, y % 2
    h2, yb = 1 - h, 3 - y
    ya = pair * 2 + (1 - side)

    def at(hh, yy, ll, xx, cc):
        return (hh * 4 + yy, (ll * 4 + xx) * 2 + cc)

    dev_a = at(h, ya, l, x, c)
    dev_b = at(h, yb, l, x, c)
    dev_z = at(h2, y, l, x, c)
    dev_d = at(h2, yb, l, x, c)
    dev_c = at(h, y, l, x, 1 - c)
    dev_x = [at(h, y, l, (x + d) % 4, c) for d in (1, 2, 3)]
    dev_l = [at(h, y, (l + d) % 4, x, c) for d in (1, 2, 3)]

    def remote(src, dst, s, r, dev):
        return pltpu.make_async_remote_copy(
            src_ref=src, dst_ref=dst, send_sem=s, recv_sem=r, device_id=dev, device_id_type=MESH
        )

    def token(tt):
        return (4 - tt) % 4

    def columns(hh, pp):
        return pl.ds(pl.multiple_of((hh * 2 + pp) * DP, DP), DP)

    def x_own(tt):
        rows = pl.ds(pl.multiple_of(token(tt) * TC, TC), TC)
        return pltpu.make_async_copy(x_hbm.at[rows, columns(h, pair)], xs.at[tt, 0, 0], sem_own.at[tt])

    def x_b(tt):
        rows = pl.ds(pl.multiple_of(token(tt) * TC + c * 64, 64), 64)
        return remote(
            x_hbm.at[rows, columns(h, 1 - pair)],
            xs.at[tt, 1, 0, pl.ds(pl.multiple_of(c * 64, 64), 64)],
            xb_s.at[tt], xb_r.at[tt], dev_b,
        )

    part = pl.ds(pl.multiple_of(c * 64 + x * 16, 16), 16)
    half = pl.ds(pl.multiple_of(c * 64, 64), 64)

    def x_z(tt):
        rows = pl.ds(pl.multiple_of(token(tt) * TC + c * 64 + x * 16, 16), 16)
        return remote(
            x_hbm.at[rows, columns(h2, pair)], xs.at[tt, 0, 1, part], xz_s.at[tt], xz_r.at[tt], dev_z
        )

    def x_d(tt):
        rows = pl.ds(pl.multiple_of(token(tt) * TC + c * 64 + x * 16, 16), 16)
        return remote(
            x_hbm.at[rows, columns(h2, 1 - pair)], xs.at[tt, 1, 1, part], xd_s.at[tt], xd_r.at[tt], dev_d
        )

    def x_x(tt, d):
        return remote(
            xs.at[tt, :, 1, part], xs.at[tt, :, 1, part], xx_s.at[tt, d], xx_r.at[tt, d], dev_x[d]
        )

    def x_c(tt):
        return remote(xs.at[tt, :, 1, half], xs.at[tt, :, 1, half], xc_s.at[tt], xc_r.at[tt], dev_c)

    def x_e(tt):
        return remote(xs.at[tt, 1, 0, half], xs.at[tt, 1, 0, half], xe_s.at[tt], xe_r.at[tt], dev_c)

    def w_rows():
        return pl.ds(pl.multiple_of(side * DB, DB), DB)

    def w_cols(f):
        return pl.ds(pl.multiple_of(f * FC, FC), FC)

    def w_own(f):
        return pltpu.make_async_copy(w_hbm.at[:, w_cols(f)], ws.at[f, w_rows()], sem_wo.at[f])

    def w_a(f):
        return remote(w_hbm.at[:, w_cols(f)], ws.at[f, w_rows()], w_s.at[f], w_r.at[f], dev_a)

    def hid_b(k):
        return remote(send_b.at[k], recv_b.at[k], b_s.at[k], b_r.at[k], dev_b)

    def hid_z(k):
        return remote(send_z.at[k], recv_z.at[k], z_s.at[k], z_r.at[k], dev_z)

    def grad_z(k):
        return remote(hg.at[k, 0, 0], hg.at[k, 0, 1], gz_s.at[k], gz_r.at[k], dev_z)

    def grad_0(k):
        return remote(hg.at[k, 0, 0], hg.at[k, 1, 0], g0_s.at[k], g0_r.at[k], dev_b)

    def grad_1(k):
        return remote(hg.at[k, 0, 1], hg.at[k, 1, 1], g1_s.at[k], g1_r.at[k], dev_b)

    def term_a(f):
        return remote(send_a.at[f], recv_a.at[f], a_s.at[f], a_r.at[f], dev_a)

    def gw_out(f):
        return pltpu.make_async_copy(gout.at[f], gw_hbm.at[:, w_cols(f)], sem_gw.at[f])

    def red_c(tt):
        return remote(send_c.at[tt], recv_c.at[tt], c_s.at[tt], c_r.at[tt], dev_c)

    def red_x(tt, d):
        return remote(send_x.at[tt, d], recv_x.at[tt, d], rx_s.at[tt, d], rx_r.at[tt, d], dev_x[d])

    def red_l(tt):
        root = token(tt)
        slot = (l - root + 4) % 4 - 1
        return remote(send_l.at[tt], recv_l.at[slot], l_s.at[tt], l_r.at[slot], at(h, y, root, x, c))

    def red_l_in(slot):
        return remote(send_l.at[0], recv_l.at[slot], l_s.at[0], l_r.at[slot], dev_l[0])

    mine = h * 2 + pair

    def final(n):
        return remote(send_f.at[n], fin.at[mine], f_s.at[n], f_r.at[n], (dev_z, dev_b, dev_d)[n])

    for tt in range(T):
        x_own(tt).start()
    for f in range(F):
        w_own(f).start()
    act_copy = pltpu.make_async_copy(act_hbm, act, sem_act)
    act_copy.start()

    barrier = pltpu.get_barrier_semaphore()
    everyone = [dev_a, dev_b, dev_z, dev_d, dev_c] + dev_x + dev_l
    for dev in everyone:
        pl.semaphore_signal(barrier, inc=1, device_id=dev, device_id_type=MESH)
    pl.semaphore_wait(barrier, len(everyone))

    w_a(0).start()
    for tt in range(2):
        x_z(tt).start()
        x_d(tt).start()
        x_b(tt).start()
    term[...] = jnp.zeros_like(term)
    for tt in range(T):
        x_own(tt).wait()
    for f in range(F):
        w_own(f).wait()
    act_copy.wait()

    def stage(step, offset, count, body):
        @pl.when((step >= offset) & (step < offset + count))
        def _():
            body(step - offset)

    def step_body(step, carry):
        def s4(k):
            hid_b(k).wait_recv()
            send_z[k] = (keep[k, 1] + recv_b[k, 1].astype(F32)).astype(BF16)
            hid_z(k).start()
            keep[k, 0] += recv_b[k, 0].astype(F32)

        stage(step, O_S4, K, s4)

        def s5(k):
            f, tt = k // T, k % T
            hid_z(k).wait_recv()
            hidden = keep[k, 0] + recv_z[k].astype(F32)
            rows = pl.ds(pl.multiple_of(token(tt) * TC, TC), TC)
            slope = gelu_slope(hidden)
            hg[k, 0, 0] = (act[rows, w_cols(f)].astype(F32) * slope).astype(BF16)
            grad_z(k).start()
            grad_0(k).start()

        stage(step, O_S5, K, s5)

        def s6(k):
            grad_z(k).wait_recv()
            grad_1(k).start()

        stage(step, O_S6, K, s6)

        def x1(tt):
            x_z(tt).wait_recv()
            x_d(tt).wait_recv()
            for d in range(3):
                x_x(tt, d).start()

            @pl.when(tt + 2 < T)
            def _():
                x_z(tt + 2).start()
                x_d(tt + 2).start()
                x_b(tt + 2).start()

        stage(step, O_X1, T, x1)

        def x2(tt):
            x_b(tt).wait_recv()
            x_e(tt).start()
            for d in range(3):
                x_x(tt, d).wait_recv()
            x_c(tt).start()

        stage(step, O_X2, T, x2)

        def s3(k):
            f, tt = k // T, k % T

            @pl.when(f == 0)
            def _():
                x_e(tt).wait_recv()
                x_c(tt).wait_recv()

            @pl.when(tt == 0)
            def _():
                w_a(f).wait_recv()

                @pl.when(f + 1 < F)
                def _():
                    w_a(f + 1).start()

            there = jnp.dot(
                xs[tt, 1].reshape(2 * TC, DP), ws[f], preferred_element_type=F32
            )
            send_b[k] = there.astype(BF16).reshape(2, TC, FC)
            hid_b(k).start()
            here = jnp.dot(
                xs[tt, 0].reshape(2 * TC, DP), ws[f], preferred_element_type=F32
            )
            keep[k] = here.reshape(2, TC, FC)

        stage(step, O_S3, K, s3)

        def s8(k):
            f, tt = k // T, k % T

            @pl.when(tt == T - 1)
            def _():
                term_a(f).wait_recv()
                own = pl.ds(pl.multiple_of(side * DB, DB), DB)
                total = (term[f, :, own] + recv_a[f].astype(F32)) * 0.125
                gout[f] = total.T
                gw_out(f).start()

        def r1(tt):
            red_c(tt).wait_recv()
            for d in range(4):
                xx = (x + d) % 4
                for blk in range(4):
                    rows = pl.ds(pl.multiple_of(blk * TC + xx * 32 + c * 16, 16), 16)
                    value = acc[rows, :] + recv_c[tt, xx, blk].astype(F32)
                    if d == 0:
                        keep_x[tt, blk] = value
                    else:
                        send_x[tt, d - 1, blk] = value.astype(BF16)
                if d:
                    red_x(tt, d - 1).start()

        stage(step, O_R1 + K - T, T, r1)

        def s7(k):
            f, tt = k // T, k % T
            grad_0(k).wait_recv()
            grad_1(k).wait_recv()
            grads = hg[k].reshape(4 * TC, FC)

            @pl.when(f == F - 1)
            def _():
                for j in range(DP // COLS):
                    cols = pl.ds(j * COLS, COLS)
                    acc[:, cols] = sum(
                        lax.dot_general(
                            hg[n * T + tt].reshape(4 * TC, FC), ws[n, cols, :],
                            (((1,), (1,)), ((), ())), preferred_element_type=F32,
                        )
                        for n in range(F)
                    )
                for xx in range(4):
                    for blk in range(4):
                        rows = pl.ds(pl.multiple_of(blk * TC + xx * 32 + (1 - c) * 16, 16), 16)
                        send_c[tt, xx, blk] = acc[rows, :].astype(BF16)
                red_c(tt).start()

            for j in range(DP // COLS):
                cols = pl.ds(j * COLS, COLS)
                term[f, :, cols] += lax.dot_general(
                    grads, xs[tt, :, :, :, cols].reshape(4 * TC, COLS),
                    (((0,), (0,)), ((), ())), preferred_element_type=F32,
                )

            @pl.when(tt == T - 1)
            def _():
                other = pl.ds(pl.multiple_of((1 - side) * DB, DB), DB)
                send_a[f] = term[f, :, other].astype(BF16)
                term_a(f).start()

        stage(step, O_S7, K, s7)
        stage(step, O_S8, K, s8)

        def r2(tt):
            for d in range(3):
                red_x(tt, d).wait_recv()
            value = keep_x[tt]
            for d in range(3):
                value = value + recv_x[tt, d].astype(F32)

            @pl.when(l == token(tt))
            def _():
                keep_l[...] = value

            @pl.when(l != token(tt))
            def _():
                send_l[tt] = value.astype(BF16)
                red_l(tt).start()

        stage(step, O_R2 + K - T, T, r2)

        def r3(tt):
            @pl.when(l == token(tt))
            def _():
                for slot in range(3):
                    red_l_in(slot).wait_recv()
                value = keep_l[...]
                for slot in range(3):
                    value = value + recv_l[slot].astype(F32)
                value = value.astype(BF16)
                fin[mine] = value[0]
                for n in range(3):
                    send_f[n] = value[n + 1]
                    final(n).start()

        stage(step, O_R3 + K - T, T, r3)
        return carry

    lax.fori_loop(0, STEPS, step_body, 0)

    for n in range(3):
        final(n).wait_recv()
    for n in range(4):
        ig_ref[:, n * DP : (n + 1) * DP] = fin[n]

    def drain_k(k, carry):
        for copy in (hid_b, hid_z, grad_z, grad_0, grad_1):
            copy(k).wait_send()
        return carry

    lax.fori_loop(0, K, drain_k, 0)

    def drain_t(tt, carry):
        for copy in (x_b, x_z, x_d, x_c, x_e, red_c):
            copy(tt).wait_send()
        for d in range(3):
            x_x(tt, d).wait_send()
            red_x(tt, d).wait_send()

        @pl.when(l != token(tt))
        def _():
            red_l(tt).wait_send()

        return carry

    lax.fori_loop(0, T, drain_t, 0)
    for f in range(F):
        w_a(f).wait_send()
        term_a(f).wait_send()
        gw_out(f).wait()
    for n in range(3):
        final(n).wait_send()


def scratch():
    dma = pltpu.SemaphoreType.DMA
    both = lambda *shape: [dma(shape), dma(shape)]
    return [
        pltpu.VMEM((T, 2, 2, TC, DP), BF16),
        pltpu.VMEM((F, DP, FC), BF16),
        pltpu.VMEM((512, 768), BF16),
        pltpu.VMEM((K, 2, TC, FC), BF16),
        pltpu.VMEM((K, 2, TC, FC), BF16),
        pltpu.VMEM((K, 2, TC, FC), F32),
        pltpu.VMEM((K, TC, FC), BF16),
        pltpu.VMEM((K, TC, FC), BF16),
        pltpu.VMEM((K, 2, 2, TC, FC), BF16),
        pltpu.VMEM((F, FC, DP), F32),
        pltpu.VMEM((4 * TC, DP), F32),
        pltpu.VMEM((T, 4, 4, 16, DP), BF16),
        pltpu.VMEM((T, 4, 4, 16, DP), BF16),
        pltpu.VMEM((T, 3, 4, 16, DP), BF16),
        pltpu.VMEM((T, 3, 4, 16, DP), BF16),
        pltpu.VMEM((T, 4, 16, DP), F32),
        pltpu.VMEM((T, 4, 16, DP), BF16),
        pltpu.VMEM((3, 4, 16, DP), BF16),
        pltpu.VMEM((4, 16, DP), F32),
        pltpu.VMEM((3, 16, DP), BF16),
        pltpu.VMEM((4, 16, DP), BF16),
        pltpu.VMEM((F, FC, DB), BF16),
        pltpu.VMEM((F, FC, DB), BF16),
        pltpu.VMEM((F, DB, FC), F32),
        dma((T,)), dma((F,)), dma, dma((F,)),
        *both(T), *both(T), *both(T), *both(T, 3), *both(T), *both(T),
        *both(F), *both(K), *both(K), *both(K), *both(K), *both(K),
        *both(F), *both(T), *both(T, 3),
        dma((T,)), dma((3,)), *both(3),
    ]


def dequant(codes, scales):
    return (codes.astype(F32) * scales.astype(F32)[:, None]).astype(BF16)


def local(inputs, act_grad, in_codes, in_scales):
    w_in = dequant(in_codes, in_scales)
    input_grad, in_grad = pl.pallas_call(
        kernel,
        out_shape=(
            jax.ShapeDtypeStruct((16, 6144), BF16),
            jax.ShapeDtypeStruct((768, 768), F32),
        ),
        in_specs=[pl.BlockSpec(memory_space=pl.ANY)] * 3,
        out_specs=(
            pl.BlockSpec(memory_space=pltpu.VMEM),
            pl.BlockSpec(memory_space=pl.ANY),
        ),
        scratch_shapes=scratch(),
        compiler_params=pltpu.CompilerParams(
            collective_id=0, has_side_effects=True, vmem_limit_bytes=60 * 1024 * 1024
        ),
        cost_estimate=pl.CostEstimate(
            flops=3 * 2 * 512 * 6144 * 768, bytes_accessed=12 * 1024 * 1024, transcendentals=512 * 768
        ),
        name="ffn_in_backward",
    )(inputs, act_grad, w_in)
    return input_grad, in_grad


def solution(mesh):
    return jax.shard_map(
        local,
        mesh=mesh,
        in_specs=(P("outer", None), P("outer", "inner"), P("outer", "inner"), P("outer")),
        out_specs=(P(("outer", "inner"), None), P("outer", "inner")),
        check_vma=False,
    )
```

time: 739 us -> 194 us (0.26)
  waiting for transfers between devices: 635 us -> 0 us
  Pallas kernels: 0 us -> 185 us
  blocking collectives: 48.5 us -> 0 us
  matrix products: 33.4 us -> 0 us
  between operations: 13.8 us -> 0.64 us
    reduce_scatter x2 -> x0, waiting for transfers between devices: 491 us -> none  [the longest x1 363 us: local(): lax.psum_scatter(term, 'outer', scatter_dimension=0, tiled=True) / n_outer]
    pallas_call x0 -> x1, Pallas kernels: none -> 185 us  [local(): pl.pallas_call(kernel, out_shape=(jax.ShapeDtypeStruct((16, 6144), BF16),...]
    all_gather x1 -> x0, waiting for transfers between devices: 143 us -> none  [local(): lax.all_gather(in_codes, 'outer', axis=0, tiled=True)]
    all_gather x1 -> x0, blocking collectives: 48.5 us -> none  [local(): lax.all_gather(in_scales, 'outer', axis=0, tiled=True)]
    dot_general x3 -> x0, matrix products: 33.4 us -> none  [the longest x1 12.5 us: local(): hidden = jnp.dot(inputs, w_in, preferred_element_type=jnp.float32)]
  transfers between devices with their start and end apart: 3 -> 0, of which waited for: 3 -> 0; matrix products, arithmetic and copies ran while one was open for 2% -> 0% of each run, Pallas kernels for 0% -> 0%
where the time goes in v1:
time: 194 us
  Pallas kernels  185 us (95%)
  local copies, waits for them, and re-layouts  4.84 us (2%)
  other arithmetic  3.23 us (2%)
    pallas_call x1, Pallas kernels, local(): pl.pallas_call(kernel, out_shape=(jax.ShapeDtypeStruct((16, 6144), BF16),...  185 us
    unnamed x2, local copies, waits for them, and re-layouts  4.84 us

profile of v1, /device:TPU:32, one launch (start us, length us, event | category | flops | bytes accessed | tf_op | source)
XLA Modules:
  0.0 193.7 jit_solution(11454608408672540235)
XLA Ops:
  0.6 0.7 convert_element_type.10
  1.3 2.5 %multiply_convert_fusion.w_hbm = bf16[768,768]{1,0:T(8,128)(2,1)} fusion(bf16[768,768]{1,0:T(8,128)(2,1)} %param.6, f32[768]{0:T(1024)S(1)} %convert_element_type.10), kind=kLoop, calls=%fused_computation | loop fusion | flops 1769472 | bytes 2362368 | tf_op jit(solution)/shard_map/convert_element_type | solution.py:449
  3.9 185.0 %ffn_in_backward.1 = (bf16[16,6144]{1,0:T(8,128)(2,1)}, f32[768,768]{1,0:T(8,128)}) custom-call(bf16[512,6144]{1,0:T(8,128)(2,1)} %x_hbm.1, bf16[512,768]{1,0:T(8,128)(2,1)} %act_hbm.1, bf16[768,768]{1,0:T(8,128)(2,1)} %multiply_convert_fusion.w_hbm), custom_call_target="tpu_custom_call" | custom-call | flops 14495514624 | bytes 12582912 | tf_op jit(solution)/shard_map/ffn_in_backward/pallas_call | solution.py:454
  188.9 1.6 copy.8
  190.5 3.2 %copy.9 = f32[768,768]{1,0:T(8,128)} copy(f32[768,768]{1,0:T(8,128)} %get-tuple-element.5) | data formatting | bytes 4718592

commit v2 on v0

v2 whole, which is shorter than its diff:
```python
import functools

import jax
import jax.numpy as jnp
from jax import lax
from jax.experimental import pallas as pl
from jax.experimental.pallas import tpu as pltpu
from jax.sharding import PartitionSpec as P

coef = 0.7978845608
cubic = 0.044715

MESH = pl.DeviceIdType.MESH
F32 = jnp.float32
BF16 = jnp.bfloat16

F = 3
T = 8
K = T * F
FC = 256
TC = 64
DB = 768
DP = 1536
COLS = 256
OWN, ACROSS, DIAGONAL, BESIDE = 0, 1, 2, 3

O_S4, O_S5, O_S6, O_S7, O_R1, O_R2, O_R3, O_S8 = 3, 6, 9, 12, 13, 16, 2, 18
STEPS = K + O_R2 + 2 * O_R3


def chunk(n):
    late = n // 12
    r = n % 6
    second = r // 4 + (1 - r // 4) * (r % 2) * (1 - r // 2 % 2)
    t = (1 - late) * (n % 4) + late * (4 + 2 * ((n - 12 * late) // 6) + second)
    f = (1 - late) * (n // 4) + late * ((r + 2) // 4) * (r - 1 - 2 * (r // 4))
    return t, f


def gelu_slope(value):
    tangent = jnp.tanh(coef * (value + cubic * value * value * value))
    return 0.5 * (1.0 + tangent) + 0.5 * value * (1.0 - tangent * tangent) * coef * (
        1.0 + 3.0 * cubic * value * value
    )


def kernel(
    x_hbm, act_hbm, codes_hbm, scales_hbm, ig_ref, gw_hbm,
    xs, ws, codes, scales, act, send_b, recv_b, keep, send_z, recv_z, hg, term,
    acc, send_c, recv_c, send_x, recv_x, keep_x, send_l, recv_l,
    send_f, fin, send_a, recv_a, gout,
    sem_own, sem_in, sem_gw,
    xb_s, xb_r, xz_s, xz_r, xd_s, xd_r, xx_s, xx_r, xc_s, xc_r,
    w_s, w_r, b_s, b_r, z_s, z_r, gz_s, gz_r, g0_s, g0_r, g1_s, g1_r,
    a_s, a_r, c_s, c_r, rx_s, rx_r, l_s, l_r, f_s, f_r,
):
    o = lax.axis_index("outer")
    i = lax.axis_index("inner")
    h, y = o // 4, o % 4
    l, x, c = i // 8, (i // 2) % 4, i % 2
    pair, side = y // 2, y % 2
    h2, yb = 1 - h, 3 - y
    ya = pair * 2 + (1 - side)

    def at(hh, yy, ll, xx, cc):
        return (hh * 4 + yy, (ll * 4 + xx) * 2 + cc)

    dev_a = at(h, ya, l, x, c)
    dev_b = at(h, yb, l, x, c)
    dev_z = at(h2, y, l, x, c)
    dev_d = at(h2, yb, l, x, c)
    dev_c = at(h, y, l, x, 1 - c)
    dev_x = [at(h, y, l, (x + d) % 4, c) for d in (1, 2, 3)]
    dev_l = [at(h, y, (l + d) % 4, x, c) for d in (1, 2, 3)]

    barrier = pltpu.get_barrier_semaphore()
    everyone = [dev_a, dev_b, dev_z, dev_d, dev_c] + dev_x + dev_l
    for dev in everyone:
        pl.semaphore_signal(barrier, inc=1, device_id=dev, device_id_type=MESH)

    def remote(src, dst, s, r, dev):
        return pltpu.make_async_remote_copy(
            src_ref=src, dst_ref=dst, send_sem=s, recv_sem=r, device_id=dev, device_id_type=MESH
        )

    def root_l(t):
        return (4 - t // 2) % 4

    def root_c(t):
        return t % 2

    def columns(hh, pp):
        return pl.ds(pl.multiple_of((hh * 2 + pp) * DP, DP), DP)

    half = pl.ds(pl.multiple_of(c * DB, DB), DB)

    def half_columns(hh, pp):
        return pl.ds(pl.multiple_of((hh * 2 + pp) * DP + c * DB, DB), DB)

    def x_own(t):
        return pltpu.make_async_copy(
            x_hbm.at[root_l(t), :, root_c(t), :, columns(h, pair)], xs.at[t, OWN], sem_own.at[t]
        )

    def x_push(t, cols, block, s, r, dev):
        return remote(
            x_hbm.at[root_l(t), x, root_c(t), :, cols], xs.at[t, block, x, :, half], s.at[t], r.at[t], dev
        )

    def x_b(t):
        return x_push(t, half_columns(h, 1 - pair), BESIDE, xb_s, xb_r, dev_b)

    def x_z(t):
        return x_push(t, half_columns(h2, pair), ACROSS, xz_s, xz_r, dev_z)

    def x_d(t):
        return x_push(t, half_columns(h2, 1 - pair), DIAGONAL, xd_s, xd_r, dev_d)

    def x_x(t, d):
        part = xs.at[t, 1:4, x, :, half]
        return remote(part, part, xx_s.at[t, d], xx_r.at[t, d], dev_x[d])

    def x_c(t):
        part = xs.at[t, 1:4, :, :, half]
        return remote(part, part, xc_s.at[t], xc_r.at[t], dev_c)

    w_rows = pl.ds(pl.multiple_of(side * DB, DB), DB)

    def f_cols(f):
        return pl.ds(pl.multiple_of(f * FC, FC), FC)

    def w_a(f):
        part = ws.at[f, w_rows]
        return remote(part, part, w_s.at[f], w_r.at[f], dev_a)

    def hid_b(k):
        return remote(send_b.at[k], recv_b.at[k], b_s.at[k], b_r.at[k], dev_b)

    def hid_z(k):
        return remote(send_z.at[k], recv_z.at[k], z_s.at[k], z_r.at[k], dev_z)

    def grad_z(k):
        return remote(hg.at[k, OWN], hg.at[k, ACROSS], gz_s.at[k], gz_r.at[k], dev_z)

    def grad_0(k):
        return remote(hg.at[k, OWN], hg.at[k, BESIDE], g0_s.at[k], g0_r.at[k], dev_b)

    def grad_1(k):
        return remote(hg.at[k, ACROSS], hg.at[k, DIAGONAL], g1_s.at[k], g1_r.at[k], dev_b)

    def term_a(f):
        return remote(send_a.at[f], recv_a.at[f], a_s.at[f], a_r.at[f], dev_a)

    def gw_out(f):
        return pltpu.make_async_copy(gout.at[f], gw_hbm.at[:, f_cols(f)], sem_gw.at[f])

    def red_c(n):
        return remote(send_c.at[n], recv_c.at[n], c_s.at[n], c_r.at[n], dev_c)

    def red_x(n, d):
        return remote(send_x.at[n, d], recv_x.at[n, d], rx_s.at[n, d], rx_r.at[n, d], dev_x[d])

    def red_up(n):
        return remote(send_l.at[n], recv_l.at[n, 0], l_s.at[n], l_r.at[n, 0], at(h, y, (l + 1) % 4, x, c))

    def red_down(n):
        return remote(send_l.at[n], recv_l.at[n, 1], l_s.at[n], l_r.at[n, 1], at(h, y, (l + 3) % 4, x, c))

    def red_send(t):
        @pl.when(l < root_l(t))
        def _():
            red_up(t // 2).start()

        @pl.when(l > root_l(t))
        def _():
            red_down(t // 2).start()

    mine = h * 2 + pair

    def final(n):
        return remote(send_f.at[n], fin.at[mine], f_s.at[n], f_r.at[n], (dev_z, dev_d, dev_b)[n])

    codes_copy = pltpu.make_async_copy(codes_hbm, codes, sem_in.at[0])
    scales_copy = pltpu.make_async_copy(scales_hbm, scales, sem_in.at[1])
    act_copy = pltpu.make_async_copy(act_hbm, act, sem_in.at[2])
    scales_copy.start()
    codes_copy.start()
    for t in range(T):
        x_own(t).start()
    act_copy.start()
    scales_copy.wait()
    codes_copy.wait()
    scale = jnp.broadcast_to(scales[...].astype(F32).reshape(1, DB), (128, DB)).T
    for f in range(F):
        for j in range(FC // 128):
            value = codes[:, f * FC + j * 128 : f * FC + (j + 1) * 128].astype(F32) * scale
            ws[f, w_rows, j * 128 : (j + 1) * 128] = value.astype(BF16)

    pl.semaphore_wait(barrier, len(everyone))

    def x_start(t):
        x_d(t).start()
        x_z(t).start()
        x_b(t).start()

    def x_share(t):
        x_b(t).wait_recv()
        x_z(t).wait_recv()
        x_d(t).wait_recv()
        for d in range(3):
            x_x(t, d).start()

    def x_core(t):
        for d in range(3):
            x_x(t, d).wait_recv()
        x_c(t).start()

    x_start(0)
    w_a(0).start()
    x_start(1)
    w_a(1).start()
    x_start(2)
    w_a(2).start()
    for t in range(3, T):
        x_start(t)
    term[...] = jnp.zeros_like(term)
    x_share(0)
    act_copy.wait()
    x_share(1)
    x_core(0)
    x_share(2)
    x_core(1)

    def stage(step, offset, body):
        @pl.when((step >= offset) & (step < offset + K))
        def _():
            t, f = chunk(step - offset)
            body(t, f, t * F + f)

    def stage_t(step, offset, body):
        @pl.when((step >= offset) & (step < offset + K))
        def _():
            t, f = chunk(step - offset)

            @pl.when(f == F - 1)
            def _():
                body(t)

    def average(f):
        term_a(f).wait_recv()
        total = term[f, :, w_rows] + recv_a[f].astype(F32)
        gout[f] = total.T
        gw_out(f).start()

    def end(t):
        return ((l == 0) & (root_l(t) > 0)) | ((l == 3) & (root_l(t) < 3))

    def step_body(step, carry):
        def s4(t, f, k):
            hid_b(k).wait_recv()
            send_z[k] = (keep[k, 1] + recv_b[k, 0].astype(F32)).astype(BF16)
            hid_z(k).start()
            keep[k, 0] += recv_b[k, 1].astype(F32)

        stage(step, O_S4, s4)

        def s5(t, f, k):
            hid_z(k).wait_recv()
            hidden = keep[k, 0] + recv_z[k].astype(F32)
            given = act[root_l(t), :, root_c(t), :, f_cols(f)].reshape(TC, FC)
            hg[k, OWN] = (given.astype(F32) * gelu_slope(hidden)).astype(BF16)
            grad_z(k).start()
            grad_0(k).start()

        stage(step, O_S5, s5)

        def s6(t, f, k):
            grad_z(k).wait_recv()
            grad_1(k).start()

        stage(step, O_S6, s6)

        @pl.when(step == 0)
        def _():
            x_share(3)

        @pl.when(step < 2)
        def _():
            x_core(step + 2)

        @pl.when((step % 2 == 0) & (step >= 4) & (step <= 10))
        def _():
            x_share((step + 4) // 2)

        @pl.when((step % 2 == 0) & (step >= 6) & (step <= 12))
        def _():
            x_core((step + 2) // 2)

        def s3(t, f, k):

            @pl.when(f == 0)
            def _():
                x_own(t).wait()
                x_c(t).wait_recv()

            @pl.when(t == 0)
            def _():
                w_a(f).wait_recv()

            both = jnp.dot(xs[t].reshape(4 * TC, DP), ws[f], preferred_element_type=F32)
            send_b[k] = both[2 * TC :].astype(BF16).reshape(2, TC, FC)
            hid_b(k).start()
            keep[k] = both[: 2 * TC].reshape(2, TC, FC)

        stage(step, 0, s3)

        def s7(t, f, k):
            grad_0(k).wait_recv()
            grad_1(k).wait_recv()
            grads = hg[k].reshape(4 * TC, FC)

            def partial(cols):
                return sum(
                    lax.dot_general(
                        hg[t * F + n].reshape(4 * TC, FC), ws[n, cols, :],
                        (((1,), (1,)), ((), ())), preferred_element_type=F32,
                    )
                    for n in range(F)
                )

            @pl.when((f == F - 1) & (c == root_c(t)))
            def _():
                for j in range(DP // COLS):
                    cols = pl.ds(j * COLS, COLS)
                    acc[t // 2, :, cols] = partial(cols)

            @pl.when((f == F - 1) & (c != root_c(t)))
            def _():
                for j in range(DP // COLS):
                    cols = pl.ds(j * COLS, COLS)
                    send_c[t // 2, :, cols] = partial(cols).astype(BF16)
                red_c(t // 2).start()

            for j in range(DP // COLS):
                cols = pl.ds(j * COLS, COLS)
                term[f, :, cols] += lax.dot_general(
                    grads, xs[t, :, :, :, cols].reshape(4 * TC, COLS),
                    (((0,), (0,)), ((), ())), preferred_element_type=F32,
                )

            @pl.when(t == T - 1)
            def _():
                other = pl.ds(pl.multiple_of((1 - side) * DB, DB), DB)
                send_a[f] = term[f, :, other].astype(BF16)
                term_a(f).start()

        stage(step, O_S7, s7)

        def r1(t):
            n = t // 2

            @pl.when(c == root_c(t))
            def _():
                red_c(n).wait_recv()
                for d in (1, 2, 3, 0):
                    xx = (x + d) % 4
                    for block in range(4):
                        rows = pl.ds(pl.multiple_of(block * TC + xx * 16, 16), 16)
                        value = acc[n, rows, :] + recv_c[n, rows, :].astype(F32)
                        if d == 0:
                            keep_x[n, block] = value
                        else:
                            send_x[n, d - 1, block] = value.astype(BF16)
                    if d:
                        red_x(n, d - 1).start()

        stage_t(step, O_R1, r1)

        def r2(t):
            n = t // 2

            @pl.when(c == root_c(t))
            def _():
                for d in range(3):
                    red_x(n, d).wait_recv()
                value = keep_x[n]
                for d in range(3):
                    value = value + recv_x[n, d].astype(F32)

                keep_x[n] = value

                @pl.when(end(t))
                def _():
                    send_l[n] = value.astype(BF16)
                    red_send(t)

        stage_t(step, O_R2, r2)

        for depth in (1, 2):

            def r3(t):
                n = t // 2

                @pl.when((c == root_c(t)) & (l < root_l(t)) & (l == depth))
                def _():
                    red_up(n).wait_recv()
                    send_l[n] = (keep_x[n] + recv_l[n, 0].astype(F32)).astype(BF16)
                    red_up(n).start()

                @pl.when((c == root_c(t)) & (l > root_l(t)) & (3 - l == depth))
                def _():
                    red_down(n).wait_recv()
                    send_l[n] = (keep_x[n] + recv_l[n, 1].astype(F32)).astype(BF16)
                    red_down(n).start()

            stage_t(step, O_R2 + O_R3 * depth, r3)

        def s8(t, f, k):
            @pl.when((t == T - 1) & (f < F - 1))
            def _():
                average(f)

        stage(step, O_S8, s8)
        return carry

    lax.fori_loop(0, STEPS, step_body, 0)

    last = (4 - l) % 4

    @pl.when(l > 0)
    def _():
        red_up(last).wait_recv()
        keep_x[last] += recv_l[last, 0].astype(F32)

    @pl.when(l < 3)
    def _():
        red_down(last).wait_recv()
        keep_x[last] += recv_l[last, 1].astype(F32)

    value = keep_x[last]
    value = value.astype(BF16)
    fin[mine] = value[OWN]
    for n in range(3):
        send_f[n] = value[n + 1]
        final(n).start()

    average(F - 1)

    def drain_k(k, carry):
        for copy in (hid_b, hid_z, grad_z, grad_0, grad_1):
            copy(k).wait_send()
        return carry

    lax.fori_loop(0, K, drain_k, 0)

    def drain_t(t, carry):
        n = t // 2
        for copy in (x_b, x_z, x_d, x_c):
            copy(t).wait_send()
        for d in range(3):
            x_x(t, d).wait_send()

        @pl.when(c != root_c(t))
        def _():
            red_c(n).wait_send()

        @pl.when(c == root_c(t))
        def _():
            for d in range(3):
                red_x(n, d).wait_send()

            @pl.when(l != root_l(t))
            def _():
                red_up(n).wait_send()

        return carry

    lax.fori_loop(0, T, drain_t, 0)
    for f in range(F):
        w_a(f).wait_send()
        term_a(f).wait_send()

    for n in range(3):
        final(n).wait_recv()
    for n in range(4):
        ig_ref[:, n * DP : (n + 1) * DP] = fin[n]
    for f in range(F):
        gw_out(f).wait()
    for n in range(3):
        final(n).wait_send()


def scratch():
    dma = pltpu.SemaphoreType.DMA
    both = lambda *shape: [dma(shape), dma(shape)]
    H = T // 2
    return [
        pltpu.VMEM((T, 4, 4, 16, DP), BF16),
        pltpu.VMEM((F, DP, FC), BF16),
        pltpu.VMEM((DB, 768), BF16),
        pltpu.VMEM((DB,), BF16),
        pltpu.VMEM((4, 4, 2, 16, 768), BF16),
        pltpu.VMEM((K, 2, TC, FC), BF16),
        pltpu.VMEM((K, 2, TC, FC), BF16),
        pltpu.VMEM((K, 2, TC, FC), F32),
        pltpu.VMEM((K, TC, FC), BF16),
        pltpu.VMEM((K, TC, FC), BF16),
        pltpu.VMEM((K, 4, TC, FC), BF16),
        pltpu.VMEM((F, FC, DP), F32),
        pltpu.VMEM((H, 4 * TC, DP), F32),
        pltpu.VMEM((H, 4 * TC, DP), BF16),
        pltpu.VMEM((H, 4 * TC, DP), BF16),
        pltpu.VMEM((H, 3, 4, 16, DP), BF16),
        pltpu.VMEM((H, 3, 4, 16, DP), BF16),
        pltpu.VMEM((H, 4, 16, DP), F32),
        pltpu.VMEM((H, 4, 16, DP), BF16),
        pltpu.VMEM((H, 2, 4, 16, DP), BF16),
        pltpu.VMEM((3, 16, DP), BF16),
        pltpu.VMEM((4, 16, DP), BF16),
        pltpu.VMEM((F, FC, DB), BF16),
        pltpu.VMEM((F, FC, DB), BF16),
        pltpu.VMEM((F, DB, FC), F32),
        dma((T,)), dma((3,)), dma((F,)),
        *both(T), *both(T), *both(T), *both(T, 3), *both(T),
        *both(F), *both(K), *both(K), *both(K), *both(K), *both(K),
        *both(F), *both(H), *both(H, 3),
        dma((H,)), dma((H, 2)), *both(3),
    ]


def local(inputs, act_grad, in_codes, in_scales):
    input_grad, in_grad = pl.pallas_call(
        kernel,
        out_shape=(
            jax.ShapeDtypeStruct((16, 6144), BF16),
            jax.ShapeDtypeStruct((768, 768), F32),
        ),
        in_specs=[pl.BlockSpec(memory_space=pl.ANY)] * 4,
        out_specs=(
            pl.BlockSpec(memory_space=pltpu.VMEM),
            pl.BlockSpec(memory_space=pl.ANY),
        ),
        scratch_shapes=scratch(),
        compiler_params=pltpu.CompilerParams(
            collective_id=0, has_side_effects=True, vmem_limit_bytes=60 * 1024 * 1024
        ),
        cost_estimate=pl.CostEstimate(
            flops=3 * 2 * 512 * 6144 * 768, bytes_accessed=12 * 1024 * 1024, transcendentals=512 * 768
        ),
        name="ffn_in_backward",
    )(
        inputs.reshape(4, 4, 2, 16, 6144),
        act_grad.reshape(4, 4, 2, 16, 768),
        in_codes,
        in_scales,
    )
    return input_grad, in_grad * 0.125


def solution(mesh):
    return jax.shard_map(
        local,
        mesh=mesh,
        in_specs=(P("outer", None), P("outer", "inner"), P("outer", "inner"), P("outer")),
        out_specs=(P(("outer", "inner"), None), P("outer", "inner")),
        check_vma=False,
    )
```

time: 739 us -> 158 us (0.21)
  waiting for transfers between devices: 635 us -> 0 us
  Pallas kernels: 0 us -> 152 us
  blocking collectives: 48.5 us -> 0 us
  matrix products: 33.4 us -> 0 us
  between operations: 13.8 us -> 0.65 us
    reduce_scatter x2 -> x0, waiting for transfers between devices: 491 us -> none  [the longest x1 363 us: local(): lax.psum_scatter(term, 'outer', scatter_dimension=0, tiled=True) / n_outer]
    pallas_call x0 -> x1, Pallas kernels: none -> 152 us  [local(): pl.pallas_call(kernel, out_shape=(jax.ShapeDtypeStruct((16, 6144), BF16),...]
    all_gather x1 -> x0, waiting for transfers between devices: 143 us -> none  [local(): lax.all_gather(in_codes, 'outer', axis=0, tiled=True)]
    all_gather x1 -> x0, blocking collectives: 48.5 us -> none  [local(): lax.all_gather(in_scales, 'outer', axis=0, tiled=True)]
    dot_general x3 -> x0, matrix products: 33.4 us -> none  [the longest x1 12.5 us: local(): hidden = jnp.dot(inputs, w_in, preferred_element_type=jnp.float32)]
  transfers between devices with their start and end apart: 3 -> 0, of which waited for: 3 -> 0; matrix products, arithmetic and copies ran while one was open for 2% -> 0% of each run, Pallas kernels for 0% -> 0%
where the time goes in v2:
time: 158 us; the launch traced here: 156 us
  Pallas kernels  152 us (96%)
  other arithmetic  3.26 us (2%)
    pallas_call x1, Pallas kernels, local(): pl.pallas_call(kernel, out_shape=(jax.ShapeDtypeStruct((16, 6144), BF16),...  152 us
    mul x1, other arithmetic, local(): return (input_grad, in_grad * 0.125)  3.26 us

profile of v2, /device:TPU:32, one launch (start us, length us, event | category | flops | bytes accessed | tf_op | source)
XLA Modules:
  0.0 156.3 jit_solution(12597302261820635446)
XLA Ops:
  0.6 151.7 %ffn_in_backward.1 = (bf16[16,6144]{1,0:T(8,128)(2,1)}, f32[768,768]{1,0:T(8,128)}) custom-call(bf16[4,4,2,16,6144]{4,3,2,1,0:T(8,128)(2,1)} %bitcast.2, bf16[4,4,2,16,768]{4,3,2,1,0:T(8,128)(2,1)} %bitcast.3, bf16[768,768]{1,0:T(8,128)(2,1)} %codes_hbm.1, bf16[768]{0:T(1024)(128)(2,1)} %scales_hbm.1), custom_call_target="tpu_custom_call" | custom-call | flops 14495514624 | bytes 12582912 | tf_op jit(solution)/shard_map/ffn_in_backward/pallas_call | solution.py:532
  152.4 0.0 copy-start
  152.4 3.3 %broadcast_multiply_fusion = f32[768,768]{1,0:T(8,128)} fusion(f32[768,768]{1,0:T(8,128)} %get-tuple-element.5), kind=kLoop, calls=%fused_computation | loop fusion | flops 589824 | bytes 4718592 | tf_op jit(solution)/shard_map/mul | solution.py:557
  155.6 0.0 copy-done
  155.6 0.7 copy.7
Async XLA Ops:
  152.4 3.3 %copy-start = (bf16[16,6144]{1,0:T(8,128)(2,1)S(1)}, bf16[16,6144]{1,0:T(8,128)(2,1)}, u32[]{:S(2)}) copy-start(bf16[16,6144]{1,0:T(8,128)(2,1)} %get-tuple-element.8) | copy-start | bytes 589828

commit v3 on v2

--- a/solution.py
+++ b/solution.py
@@ -24,7 +24,7 @@
 COLS = 256
 OWN, ACROSS, DIAGONAL, BESIDE = 0, 1, 2, 3
 
-O_S4, O_S5, O_S6, O_S7, O_R1, O_R2, O_R3, O_S8 = 3, 6, 9, 12, 13, 16, 2, 18
+O_S4, O_S5, O_S6, O_S7, O_R1, O_R2, O_R3 = 3, 6, 9, 12, 13, 19, 3
 STEPS = K + O_R2 + 2 * O_R3
 
 
@@ -45,13 +45,13 @@
 
 
 def kernel(
-    x_hbm, act_hbm, codes_hbm, scales_hbm, ig_ref, gw_hbm,
+    x_hbm, act_hbm, codes_hbm, scales_hbm, ig_hbm, gw_hbm,
     xs, ws, codes, scales, act, send_b, recv_b, keep, send_z, recv_z, hg, term,
     acc, send_c, recv_c, send_x, recv_x, keep_x, send_l, recv_l,
     send_f, fin, send_a, recv_a, gout,
-    sem_own, sem_in, sem_gw,
-    xb_s, xb_r, xz_s, xz_r, xd_s, xd_r, xx_s, xx_r, xc_s, xc_r,
-    w_s, w_r, b_s, b_r, z_s, z_r, gz_s, gz_r, g0_s, g0_r, g1_s, g1_r,
+    sem_own, sem_in, sem_gw, sem_ig,
+    xb_s, xz_s, xd_s, xp_r, xx_s, xx_r, xc_s, xc_r,
+    w_s, w_r, b_s, b_r, z_s, z_r, gz_s, gz_r, g0_s, g1_s, g_r,
     a_s, a_r, c_s, c_r, rx_s, rx_r, l_s, l_r, f_s, f_r,
 ):
     o = lax.axis_index("outer")
@@ -99,30 +99,30 @@
 
     def x_own(t):
         return pltpu.make_async_copy(
-            x_hbm.at[root_l(t), :, root_c(t), :, columns(h, pair)], xs.at[t, OWN], sem_own.at[t]
+            x_hbm.at[root_l(t), :, root_c(t), :, columns(h, pair)], xs.at[t, OWN], sem_own
         )
 
-    def x_push(t, cols, block, s, r, dev):
+    def x_push(t, cols, block, s, dev):
         return remote(
-            x_hbm.at[root_l(t), x, root_c(t), :, cols], xs.at[t, block, x, :, half], s.at[t], r.at[t], dev
+            x_hbm.at[root_l(t), x, root_c(t), :, cols], xs.at[t, block, x, :, half], s, xp_r.at[t], dev
         )
 
     def x_b(t):
-        return x_push(t, half_columns(h, 1 - pair), BESIDE, xb_s, xb_r, dev_b)
+        return x_push(t, half_columns(h, 1 - pair), BESIDE, xb_s, dev_b)
 
     def x_z(t):
-        return x_push(t, half_columns(h2, pair), ACROSS, xz_s, xz_r, dev_z)
+        return x_push(t, half_columns(h2, pair), ACROSS, xz_s, dev_z)
 
     def x_d(t):
-        return x_push(t, half_columns(h2, 1 - pair), DIAGONAL, xd_s, xd_r, dev_d)
+        return x_push(t, half_columns(h2, 1 - pair), DIAGONAL, xd_s, dev_d)
 
     def x_x(t, d):
         part = xs.at[t, 1:4, x, :, half]
-        return remote(part, part, xx_s.at[t, d], xx_r.at[t, d], dev_x[d])
+        return remote(part, part, xx_s.at[d], xx_r.at[t], dev_x[d])
 
     def x_c(t):
         part = xs.at[t, 1:4, :, :, half]
-        return remote(part, part, xc_s.at[t], xc_r.at[t], dev_c)
+        return remote(part, part, xc_s, xc_r.at[t], dev_c)
 
     w_rows = pl.ds(pl.multiple_of(side * DB, DB), DB)
 
@@ -131,40 +131,40 @@
 
     def w_a(f):
         part = ws.at[f, w_rows]
-        return remote(part, part, w_s.at[f], w_r.at[f], dev_a)
+        return remote(part, part, w_s, w_r.at[f], dev_a)
 
     def hid_b(k):
-        return remote(send_b.at[k], recv_b.at[k], b_s.at[k], b_r.at[k], dev_b)
+        return remote(send_b.at[k], recv_b.at[k], b_s, b_r.at[k], dev_b)
 
     def hid_z(k):
-        return remote(send_z.at[k], recv_z.at[k], z_s.at[k], z_r.at[k], dev_z)
+        return remote(send_z.at[k], recv_z.at[k], z_s, z_r.at[k], dev_z)
 
     def grad_z(k):
-        return remote(hg.at[k, OWN], hg.at[k, ACROSS], gz_s.at[k], gz_r.at[k], dev_z)
+        return remote(hg.at[k, OWN], hg.at[k, ACROSS], gz_s, gz_r.at[k], dev_z)
 
     def grad_0(k):
-        return remote(hg.at[k, OWN], hg.at[k, BESIDE], g0_s.at[k], g0_r.at[k], dev_b)
+        return remote(hg.at[k, OWN], hg.at[k, BESIDE], g0_s, g_r.at[k], dev_b)
 
     def grad_1(k):
-        return remote(hg.at[k, ACROSS], hg.at[k, DIAGONAL], g1_s.at[k], g1_r.at[k], dev_b)
+        return remote(hg.at[k, ACROSS], hg.at[k, DIAGONAL], g1_s, g_r.at[k], dev_b)
 
     def term_a(f):
-        return remote(send_a.at[f], recv_a.at[f], a_s.at[f], a_r.at[f], dev_a)
+        return remote(send_a.at[f], recv_a.at[f], a_s, a_r.at[f], dev_a)
 
     def gw_out(f):
-        return pltpu.make_async_copy(gout.at[f], gw_hbm.at[:, f_cols(f)], sem_gw.at[f])
+        return pltpu.make_async_copy(gout.at[f], gw_hbm.at[:, f_cols(f)], sem_gw)
 
     def red_c(n):
-        return remote(send_c.at[n], recv_c.at[n], c_s.at[n], c_r.at[n], dev_c)
+        return remote(send_c.at[n], recv_c.at[n], c_s, c_r.at[n], dev_c)
 
     def red_x(n, d):
-        return remote(send_x.at[n, d], recv_x.at[n, d], rx_s.at[n, d], rx_r.at[n, d], dev_x[d])
+        return remote(send_x.at[n, d], recv_x.at[n, d], rx_s.at[d], rx_r.at[n], dev_x[d])
 
     def red_up(n):
-        return remote(send_l.at[n], recv_l.at[n, 0], l_s.at[n], l_r.at[n, 0], at(h, y, (l + 1) % 4, x, c))
+        return remote(send_l.at[n], recv_l.at[n, 0], l_s, l_r.at[n, 0], at(h, y, (l + 1) % 4, x, c))
 
     def red_down(n):
-        return remote(send_l.at[n], recv_l.at[n, 1], l_s.at[n], l_r.at[n, 1], at(h, y, (l + 3) % 4, x, c))
+        return remote(send_l.at[n], recv_l.at[n, 1], l_s, l_r.at[n, 1], at(h, y, (l + 3) % 4, x, c))
 
     def red_send(t):
         @pl.when(l < root_l(t))
@@ -178,7 +178,10 @@
     mine = h * 2 + pair
 
     def final(n):
-        return remote(send_f.at[n], fin.at[mine], f_s.at[n], f_r.at[n], (dev_z, dev_d, dev_b)[n])
+        return remote(send_f.at[n], fin.at[mine], f_s, f_r, (dev_z, dev_d, dev_b)[n])
+
+    def ig_out(n):
+        return pltpu.make_async_copy(fin.at[n], ig_hbm.at[:, n * DP : (n + 1) * DP], sem_ig)
 
     codes_copy = pltpu.make_async_copy(codes_hbm, codes, sem_in.at[0])
     scales_copy = pltpu.make_async_copy(scales_hbm, scales, sem_in.at[1])
@@ -204,15 +207,14 @@
         x_b(t).start()
 
     def x_share(t):
-        x_b(t).wait_recv()
-        x_z(t).wait_recv()
-        x_d(t).wait_recv()
+        part = xs.at[t, 1:4, x, :, half]
+        remote(part, part, xc_s, xp_r.at[t], dev_c).wait_recv()
         for d in range(3):
             x_x(t, d).start()
 
     def x_core(t):
-        for d in range(3):
-            x_x(t, d).wait_recv()
+        part = xs.at[t, 1:4, 0:3, :, half]
+        remote(part, part, xc_s, xx_r.at[t], dev_c).wait_recv()
         x_c(t).start()
 
     x_start(0)
@@ -226,6 +228,7 @@
     term[...] = jnp.zeros_like(term)
     x_share(0)
     act_copy.wait()
+    pltpu.make_async_copy(xs.at[:, OWN], xs.at[:, OWN], sem_own).wait()
     x_share(1)
     x_core(0)
     x_share(2)
@@ -280,27 +283,10 @@
 
         stage(step, O_S6, s6)
 
-        @pl.when(step == 0)
-        def _():
-            x_share(3)
-
-        @pl.when(step < 2)
-        def _():
-            x_core(step + 2)
-
-        @pl.when((step % 2 == 0) & (step >= 4) & (step <= 10))
-        def _():
-            x_share((step + 4) // 2)
-
-        @pl.when((step % 2 == 0) & (step >= 6) & (step <= 12))
-        def _():
-            x_core((step + 2) // 2)
-
         def s3(t, f, k):
 
             @pl.when(f == 0)
             def _():
-                x_own(t).wait()
                 x_c(t).wait_recv()
 
             @pl.when(t == 0)
@@ -314,9 +300,25 @@
 
         stage(step, 0, s3)
 
+        @pl.when(step == 0)
+        def _():
+            x_share(3)
+
+        @pl.when(step < 2)
+        def _():
+            x_core(step + 2)
+
+        @pl.when((step % 2 == 0) & (step >= 4) & (step <= 10))
+        def _():
+            x_share((step + 4) // 2)
+
+        @pl.when((step % 2 == 0) & (step >= 6) & (step <= 12))
+        def _():
+            x_core((step + 2) // 2)
+
         def s7(t, f, k):
-            grad_0(k).wait_recv()
-            grad_1(k).wait_recv()
+            beside = hg.at[k, 2:4]
+            remote(beside, beside, g0_s, g_r.at[k], dev_b).wait_recv()
             grads = hg[k].reshape(4 * TC, FC)
 
             def partial(cols):
@@ -381,8 +383,7 @@
 
             @pl.when(c == root_c(t))
             def _():
-                for d in range(3):
-                    red_x(n, d).wait_recv()
+                remote(send_x.at[n], recv_x.at[n], rx_s.at[0], rx_r.at[n], dev_c).wait_recv()
                 value = keep_x[n]
                 for d in range(3):
                     value = value + recv_x[n, d].astype(F32)
@@ -415,15 +416,12 @@
 
             stage_t(step, O_R2 + O_R3 * depth, r3)
 
-        def s8(t, f, k):
-            @pl.when((t == T - 1) & (f < F - 1))
-            def _():
-                average(f)
-
-        stage(step, O_S8, s8)
         return carry
 
     lax.fori_loop(0, STEPS, step_body, 0)
+
+    for f in range(F - 1):
+        average(f)
 
     last = (4 - l) % 4
 
@@ -446,53 +444,36 @@
 
     average(F - 1)
 
-    def drain_k(k, carry):
-        for copy in (hid_b, hid_z, grad_z, grad_0, grad_1):
-            copy(k).wait_send()
-        return carry
-
-    lax.fori_loop(0, K, drain_k, 0)
-
-    def drain_t(t, carry):
-        n = t // 2
-        for copy in (x_b, x_z, x_d, x_c):
-            copy(t).wait_send()
-        for d in range(3):
-            x_x(t, d).wait_send()
-
-        @pl.when(c != root_c(t))
-        def _():
-            red_c(n).wait_send()
-
-        @pl.when(c == root_c(t))
-        def _():
-            for d in range(3):
-                red_x(n, d).wait_send()
-
-            @pl.when(l != root_l(t))
-            def _():
-                red_up(n).wait_send()
-
-        return carry
-
-    lax.fori_loop(0, T, drain_t, 0)
-    for f in range(F):
-        w_a(f).wait_send()
-        term_a(f).wait_send()
-
-    for n in range(3):
-        final(n).wait_recv()
+    def left(buffer, s):
+        remote(buffer, buffer, s, f_r, dev_c).wait_send()
+
+    pushed = xs.at[:, BESIDE, x, :, half]
+    for s in (xb_s, xz_s, xd_s):
+        left(pushed, s)
+    for d in range(3):
+        left(xs.at[:, 1:4, x, :, half], xx_s.at[d])
+        left(send_x.at[:, d], rx_s.at[d])
+    left(xs.at[:, 1:4, :, :, half], xc_s)
+    left(ws.at[:, w_rows], w_s)
+    left(send_b, b_s)
+    left(send_z, z_s)
+    left(hg.at[:, OWN], gz_s)
+    left(hg.at[:, OWN], g0_s)
+    left(hg.at[:, ACROSS], g1_s)
+    left(send_a, a_s)
+    left(send_c, c_s)
+    left(send_l.at[0:3], l_s)
+    left(send_f, f_s)
+
+    remote(fin.at[0:3], fin.at[0:3], f_s, f_r, dev_c).wait_recv()
     for n in range(4):
-        ig_ref[:, n * DP : (n + 1) * DP] = fin[n]
-    for f in range(F):
-        gw_out(f).wait()
-    for n in range(3):
-        final(n).wait_send()
+        ig_out(n).start()
+    pltpu.make_async_copy(gout, gout, sem_gw).wait()
+    pltpu.make_async_copy(fin, fin, sem_ig).wait()
 
 
 def scratch():
     dma = pltpu.SemaphoreType.DMA
-    both = lambda *shape: [dma(shape), dma(shape)]
     H = T // 2
     return [
         pltpu.VMEM((T, 4, 4, 16, DP), BF16),
@@ -520,11 +501,10 @@
         pltpu.VMEM((F, FC, DB), BF16),
         pltpu.VMEM((F, FC, DB), BF16),
         pltpu.VMEM((F, DB, FC), F32),
-        dma((T,)), dma((3,)), dma((F,)),
-        *both(T), *both(T), *both(T), *both(T, 3), *both(T),
-        *both(F), *both(K), *both(K), *both(K), *both(K), *both(K),
-        *both(F), *both(H), *both(H, 3),
-        dma((H,)), dma((H, 2)), *both(3),
+        dma, dma((3,)), dma, dma,
+        dma, dma, dma, dma((T,)), dma((3,)), dma((T,)), dma, dma((T,)),
+        dma, dma((F,)), dma, dma((K,)), dma, dma((K,)), dma, dma((K,)), dma, dma, dma((K,)),
+        dma, dma((F,)), dma, dma((H,)), dma((3,)), dma((H,)), dma, dma((H, 2)), dma, dma,
     ]
 
 
@@ -537,7 +517,7 @@
         ),
         in_specs=[pl.BlockSpec(memory_space=pl.ANY)] * 4,
         out_specs=(
-            pl.BlockSpec(memory_space=pltpu.VMEM),
+            pl.BlockSpec(memory_space=pl.ANY),
             pl.BlockSpec(memory_space=pl.ANY),
         ),
         scratch_shapes=scratch(),

time: 158 us -> 150 us (0.949)
  Pallas kernels: 152 us -> 144 us
    pallas_call x1, Pallas kernels: 152 us -> 144 us  [local(): pl.pallas_call(kernel, out_shape=(jax.ShapeDtypeStruct((16, 6144), BF16),...]
where the time goes in v3:
time: 150 us; the launch traced here: 149 us
  Pallas kernels  144 us (96%)
  other arithmetic  3.26 us (2%)
    pallas_call x1, Pallas kernels, local(): pl.pallas_call(kernel, out_shape=(jax.ShapeDtypeStruct((16, 6144), BF16),...  144 us
    mul x1, other arithmetic, local(): return (input_grad, in_grad * 0.125)  3.26 us

profile of v3, /device:TPU:32, one launch (start us, length us, event | category | flops | bytes accessed | tf_op | source)
XLA Modules:
  0.0 149.0 jit_solution(12265242536647009444)
XLA Ops:
  0.6 144.4 %ffn_in_backward.1 = (bf16[16,6144]{1,0:T(8,128)(2,1)}, f32[768,768]{1,0:T(8,128)}) custom-call(bf16[4,4,2,16,6144]{4,3,2,1,0:T(8,128)(2,1)} %bitcast.2, bf16[4,4,2,16,768]{4,3,2,1,0:T(8,128)(2,1)} %bitcast.3, bf16[768,768]{1,0:T(8,128)(2,1)} %codes_hbm.1, bf16[768]{0:T(1024)(128)(2,1)} %scales_hbm.1), custom_call_target="tpu_custom_call" | custom-call | flops 14495514624 | bytes 12582912 | tf_op jit(solution)/shard_map/ffn_in_backward/pallas_call | solution.py:512
  145.1 0.0 copy-start
  145.1 3.3 %broadcast_multiply_fusion = f32[768,768]{1,0:T(8,128)} fusion(f32[768,768]{1,0:T(8,128)} %get-tuple-element.5), kind=kLoop, calls=%fused_computation | loop fusion | flops 589824 | bytes 4718592 | tf_op jit(solution)/shard_map/mul | solution.py:537
  148.3 0.0 copy-done
  148.3 0.7 copy.7
Async XLA Ops:
  145.1 3.3 %copy-start = (bf16[16,6144]{1,0:T(8,128)(2,1)S(1)}, bf16[16,6144]{1,0:T(8,128)(2,1)}, u32[]{:S(2)}) copy-start(bf16[16,6144]{1,0:T(8,128)(2,1)} %get-tuple-element.8) | copy-start | bytes 589828

commit v4 on v3

--- a/solution.py
+++ b/solution.py
@@ -15,7 +15,8 @@
 BF16 = jnp.bfloat16
 
 F = 3
-T = 8
+H = 4
+T = 2 * H
 K = T * F
 FC = 256
 TC = 64
@@ -47,12 +48,12 @@
 def kernel(
     x_hbm, act_hbm, codes_hbm, scales_hbm, ig_hbm, gw_hbm,
     xs, ws, codes, scales, act, send_b, recv_b, keep, send_z, recv_z, hg, term,
-    acc, send_c, recv_c, send_x, recv_x, keep_x, send_l, recv_l,
+    acc, send_c, recv_c, send_x, recv_x, keep_x, send_l, recv_l, recv_f,
     send_f, fin, send_a, recv_a, gout,
     sem_own, sem_in, sem_gw, sem_ig,
     xb_s, xz_s, xd_s, xp_r, xx_s, xx_r, xc_s, xc_r,
     w_s, w_r, b_s, b_r, z_s, z_r, gz_s, gz_r, g0_s, g1_s, g_r,
-    a_s, a_r, c_s, c_r, rx_s, rx_r, l_s, l_r, f_s, f_r,
+    a_s, a_r, c_s, c_r, rx_s, rx_r, l_s, l_r, lf_r, f_s, f_r,
 ):
     o = lax.axis_index("outer")
     i = lax.axis_index("inner")
@@ -84,10 +85,10 @@
         )
 
     def root_l(t):
-        return (4 - t // 2) % 4
+        return (1 - t // 4) * 3 * (t // 2) + t // 4 * (1 + t % 2)
 
     def root_c(t):
-        return t % 2
+        return t % 2 + t // 6 * (1 - 2 * (t % 2))
 
     def columns(hh, pp):
         return pl.ds(pl.multiple_of((hh * 2 + pp) * DP, DP), DP)
@@ -166,14 +167,23 @@
     def red_down(n):
         return remote(send_l.at[n], recv_l.at[n, 1], l_s, l_r.at[n, 1], at(h, y, (l + 3) % 4, x, c))
 
+    def red_far(n):
+        return remote(send_l.at[n], recv_f, l_s, lf_r, at(h, y, (l + 2) % 4, x, c))
+
     def red_send(t):
-        @pl.when(l < root_l(t))
+        far = (t // 2 == H - 1) & (((l == 3) & (root_l(t) == 1)) | ((l == 0) & (root_l(t) == 2)))
+
+        @pl.when((l > root_l(t)) & jnp.logical_not(far))
+        def _():
+            red_down(t // 2).start()
+
+        @pl.when((l < root_l(t)) & jnp.logical_not(far))
         def _():
             red_up(t // 2).start()
 
-        @pl.when(l > root_l(t))
-        def _():
-            red_down(t // 2).start()
+        @pl.when(far)
+        def _():
+            red_far(t // 2).start()
 
     mine = h * 2 + pair
 
@@ -191,6 +201,26 @@
     for t in range(T):
         x_own(t).start()
     act_copy.start()
+    pl.semaphore_wait(barrier, len(everyone))
+
+    def x_start(t):
+        x_d(t).start()
+        x_z(t).start()
+        x_b(t).start()
+
+    def x_share(t):
+        part = xs.at[t, 1:4, x, :, half]
+        remote(part, part, xc_s, xp_r.at[t], dev_c).wait_recv()
+        for d in range(3):
+            x_x(t, d).start()
+
+    def x_core(t):
+        part = xs.at[t, 1:4, 0:3, :, half]
+        remote(part, part, xc_s, xx_r.at[t], dev_c).wait_recv()
+        x_c(t).start()
+
+    x_start(0)
+    x_start(1)
     scales_copy.wait()
     codes_copy.wait()
     scale = jnp.broadcast_to(scales[...].astype(F32).reshape(1, DB), (128, DB)).T
@@ -198,28 +228,7 @@
         for j in range(FC // 128):
             value = codes[:, f * FC + j * 128 : f * FC + (j + 1) * 128].astype(F32) * scale
             ws[f, w_rows, j * 128 : (j + 1) * 128] = value.astype(BF16)
-
-    pl.semaphore_wait(barrier, len(everyone))
-
-    def x_start(t):
-        x_d(t).start()
-        x_z(t).start()
-        x_b(t).start()
-
-    def x_share(t):
-        part = xs.at[t, 1:4, x, :, half]
-        remote(part, part, xc_s, xp_r.at[t], dev_c).wait_recv()
-        for d in range(3):
-            x_x(t, d).start()
-
-    def x_core(t):
-        part = xs.at[t, 1:4, 0:3, :, half]
-        remote(part, part, xc_s, xx_r.at[t], dev_c).wait_recv()
-        x_c(t).start()
-
-    x_start(0)
     w_a(0).start()
-    x_start(1)
     w_a(1).start()
     x_start(2)
     w_a(2).start()
@@ -256,7 +265,7 @@
         gw_out(f).start()
 
     def end(t):
-        return ((l == 0) & (root_l(t) > 0)) | ((l == 3) & (root_l(t) < 3))
+        return ((l == 0) & (root_l(t) > 0)) | ((l == 3) & (root_l(t) < 3)) | ((l != root_l(t)) & (t // 2 == H - 1))
 
     def step_body(step, carry):
         def s4(t, f, k):
@@ -315,48 +324,6 @@
         @pl.when((step % 2 == 0) & (step >= 6) & (step <= 12))
         def _():
             x_core((step + 2) // 2)
-
-        def s7(t, f, k):
-            beside = hg.at[k, 2:4]
-            remote(beside, beside, g0_s, g_r.at[k], dev_b).wait_recv()
-            grads = hg[k].reshape(4 * TC, FC)
-
-            def partial(cols):
-                return sum(
-                    lax.dot_general(
-                        hg[t * F + n].reshape(4 * TC, FC), ws[n, cols, :],
-                        (((1,), (1,)), ((), ())), preferred_element_type=F32,
-                    )
-                    for n in range(F)
-                )
-
-            @pl.when((f == F - 1) & (c == root_c(t)))
-            def _():
-                for j in range(DP // COLS):
-                    cols = pl.ds(j * COLS, COLS)
-                    acc[t // 2, :, cols] = partial(cols)
-
-            @pl.when((f == F - 1) & (c != root_c(t)))
-            def _():
-                for j in range(DP // COLS):
-                    cols = pl.ds(j * COLS, COLS)
-                    send_c[t // 2, :, cols] = partial(cols).astype(BF16)
-                red_c(t // 2).start()
-
-            for j in range(DP // COLS):
-                cols = pl.ds(j * COLS, COLS)
-                term[f, :, cols] += lax.dot_general(
-                    grads, xs[t, :, :, :, cols].reshape(4 * TC, COLS),
-                    (((0,), (0,)), ((), ())), preferred_element_type=F32,
-                )
-
-            @pl.when(t == T - 1)
-            def _():
-                other = pl.ds(pl.multiple_of((1 - side) * DB, DB), DB)
-                send_a[f] = term[f, :, other].astype(BF16)
-                term_a(f).start()
-
-        stage(step, O_S7, s7)
 
         def r1(t):
             n = t // 2
@@ -378,6 +345,48 @@
 
         stage_t(step, O_R1, r1)
 
+        def s7(t, f, k):
+            beside = hg.at[k, 2:4]
+            remote(beside, beside, g0_s, g_r.at[k], dev_b).wait_recv()
+            grads = hg[k].reshape(4 * TC, FC)
+
+            def partial(cols):
+                return sum(
+                    lax.dot_general(
+                        hg[t * F + n].reshape(4 * TC, FC), ws[n, cols, :],
+                        (((1,), (1,)), ((), ())), preferred_element_type=F32,
+                    )
+                    for n in range(F)
+                )
+
+            @pl.when((f == F - 1) & (c == root_c(t)))
+            def _():
+                for j in range(DP // COLS):
+                    cols = pl.ds(j * COLS, COLS)
+                    acc[t // 2, :, cols] = partial(cols)
+
+            @pl.when((f == F - 1) & (c != root_c(t)))
+            def _():
+                for j in range(DP // COLS):
+                    cols = pl.ds(j * COLS, COLS)
+                    send_c[t // 2, :, cols] = partial(cols).astype(BF16)
+                red_c(t // 2).start()
+
+            for j in range(DP // COLS):
+                cols = pl.ds(j * COLS, COLS)
+                term[f, :, cols] += lax.dot_general(
+                    grads, xs[t, :, :, :, cols].reshape(4 * TC, COLS),
+                    (((0,), (0,)), ((), ())), preferred_element_type=F32,
+                )
+
+            @pl.when(t == T - 1)
+            def _():
+                other = pl.ds(pl.multiple_of((1 - side) * DB, DB), DB)
+                send_a[f] = term[f, :, other].astype(BF16)
+                term_a(f).start()
+
+        stage(step, O_S7, s7)
+
         def r2(t):
             n = t // 2
 
@@ -402,13 +411,13 @@
             def r3(t):
                 n = t // 2
 
-                @pl.when((c == root_c(t)) & (l < root_l(t)) & (l == depth))
+                @pl.when((c == root_c(t)) & (l < root_l(t)) & (l == depth) & (n < H - 1))
                 def _():
                     red_up(n).wait_recv()
                     send_l[n] = (keep_x[n] + recv_l[n, 0].astype(F32)).astype(BF16)
                     red_up(n).start()
 
-                @pl.when((c == root_c(t)) & (l > root_l(t)) & (3 - l == depth))
+                @pl.when((c == root_c(t)) & (l > root_l(t)) & (3 - l == depth) & (n < H - 1))
                 def _():
                     red_down(n).wait_recv()
                     send_l[n] = (keep_x[n] + recv_l[n, 1].astype(F32)).astype(BF16)
@@ -423,7 +432,7 @@
     for f in range(F - 1):
         average(f)
 
-    last = (4 - l) % 4
+    last = l // 3 + (l + 1) // 2 % 2 * (2 + (l + c + 1) % 2)
 
     @pl.when(l > 0)
     def _():
@@ -434,6 +443,11 @@
     def _():
         red_down(last).wait_recv()
         keep_x[last] += recv_l[last, 1].astype(F32)
+
+    @pl.when(last == H - 1)
+    def _():
+        red_far(last).wait_recv()
+        keep_x[last] += recv_f[...].astype(F32)
 
     value = keep_x[last]
     value = value.astype(BF16)
@@ -474,7 +488,6 @@
 
 def scratch():
     dma = pltpu.SemaphoreType.DMA
-    H = T // 2
     return [
         pltpu.VMEM((T, 4, 4, 16, DP), BF16),
         pltpu.VMEM((F, DP, FC), BF16),
@@ -496,6 +509,7 @@
         pltpu.VMEM((H, 4, 16, DP), F32),
         pltpu.VMEM((H, 4, 16, DP), BF16),
         pltpu.VMEM((H, 2, 4, 16, DP), BF16),
+        pltpu.VMEM((4, 16, DP), BF16),
         pltpu.VMEM((3, 16, DP), BF16),
         pltpu.VMEM((4, 16, DP), BF16),
         pltpu.VMEM((F, FC, DB), BF16),
@@ -504,7 +518,7 @@
         dma, dma((3,)), dma, dma,
         dma, dma, dma, dma((T,)), dma((3,)), dma((T,)), dma, dma((T,)),
         dma, dma((F,)), dma, dma((K,)), dma, dma((K,)), dma, dma((K,)), dma, dma, dma((K,)),
-        dma, dma((F,)), dma, dma((H,)), dma((3,)), dma((H,)), dma, dma((H, 2)), dma, dma,
+        dma, dma((F,)), dma, dma((H,)), dma((3,)), dma((H,)), dma, dma((H, 2)), dma, dma, dma,
     ]
 
 

time: 150 us -> 143 us (0.953)
  the two profiles are of different devices: /device:TPU:32 before, /device:TPU:88 now
where the time goes in v4:
time: 143 us
  Pallas kernels  139 us (97%)
  other arithmetic  3.26 us (2%)
    pallas_call x1, Pallas kernels, local(): pl.pallas_call(kernel, out_shape=(jax.ShapeDtypeStruct((16, 6144), BF16),...  139 us
    mul x1, other arithmetic, local(): return (input_grad, in_grad * 0.125)  3.26 us

profile of v4, /device:TPU:88, one launch (start us, length us, event | category | flops | bytes accessed | tf_op | source)
XLA Modules:
  0.0 143.3 jit_solution(13967484631207632611)
XLA Ops:
  0.6 138.8 %ffn_in_backward.1 = (bf16[16,6144]{1,0:T(8,128)(2,1)}, f32[768,768]{1,0:T(8,128)}) custom-call(bf16[4,4,2,16,6144]{4,3,2,1,0:T(8,128)(2,1)} %bitcast.2, bf16[4,4,2,16,768]{4,3,2,1,0:T(8,128)(2,1)} %bitcast.3, bf16[768,768]{1,0:T(8,128)(2,1)} %codes_hbm.1, bf16[768]{0:T(1024)(128)(2,1)} %scales_hbm.1), custom_call_target="tpu_custom_call" | custom-call | flops 14495514624 | bytes 12582912 | tf_op jit(solution)/shard_map/ffn_in_backward/pallas_call | solution.py:526
  139.4 0.0 copy-start
  139.4 3.3 %broadcast_multiply_fusion = f32[768,768]{1,0:T(8,128)} fusion(f32[768,768]{1,0:T(8,128)} %get-tuple-element.5), kind=kLoop, calls=%fused_computation | loop fusion | flops 589824 | bytes 4718592 | tf_op jit(solution)/shard_map/mul | solution.py:551
  142.7 0.0 copy-done
  142.7 0.7 copy.7
Async XLA Ops:
  139.4 3.3 %copy-start = (bf16[16,6144]{1,0:T(8,128)(2,1)S(1)}, bf16[16,6144]{1,0:T(8,128)(2,1)}, u32[]{:S(2)}) copy-start(bf16[16,6144]{1,0:T(8,128)(2,1)} %get-tuple-element.8) | copy-start | bytes 589828

commit v5 on v4

--- a/solution.py
+++ b/solution.py
@@ -23,19 +23,22 @@
 DB = 768
 DP = 1536
 COLS = 256
+HALVES = (slice(0, DB), slice(DB, DP))
 OWN, ACROSS, DIAGONAL, BESIDE = 0, 1, 2, 3
 
-O_S4, O_S5, O_S6, O_S7, O_R1, O_R2, O_R3 = 3, 6, 9, 12, 13, 19, 3
-STEPS = K + O_R2 + 2 * O_R3
+O_S4, O_S5, O_S6, O_S7, O_R1, O_R2 = 3, 6, 9, 12, 13, 24
+STEPS = K + O_R2
 
 
 def chunk(n):
     late = n // 12
-    r = n % 6
-    second = r // 4 + (1 - r // 4) * (r % 2) * (1 - r // 2 % 2)
-    t = (1 - late) * (n % 4) + late * (4 + 2 * ((n - 12 * late) // 6) + second)
-    f = (1 - late) * (n // 4) + late * ((r + 2) // 4) * (r - 1 - 2 * (r // 4))
-    return t, f
+    r = n % 12
+    e = r // 6
+    q = r % 6
+    s = q // 2
+    t = 4 + (1 - e) * (s // 2 * 2 + (1 - s % 2) * (q % 2)) + e * (1 + s)
+    f = (1 - e) * (s % 2) * (1 + q % 2) + e * (1 + q % 2)
+    return (1 - late) * (r % 4) + late * t, (1 - late) * (r // 4) + late * f
 
 
 def gelu_slope(value):
@@ -48,12 +51,12 @@
 def kernel(
     x_hbm, act_hbm, codes_hbm, scales_hbm, ig_hbm, gw_hbm,
     xs, ws, codes, scales, act, send_b, recv_b, keep, send_z, recv_z, hg, term,
-    acc, send_c, recv_c, send_x, recv_x, keep_x, send_l, recv_l, recv_f,
+    acc, send_c, recv_c, send_x, recv_x, keep_x, send_l, recv_l,
     send_f, fin, send_a, recv_a, gout,
     sem_own, sem_in, sem_gw, sem_ig,
     xb_s, xz_s, xd_s, xp_r, xx_s, xx_r, xc_s, xc_r,
     w_s, w_r, b_s, b_r, z_s, z_r, gz_s, gz_r, g0_s, g1_s, g_r,
-    a_s, a_r, c_s, c_r, rx_s, rx_r, l_s, l_r, lf_r, f_s, f_r,
+    a_s, a_r, c_s, c_r, rx_s, rx_r, l_s, l_r, f_s, f_r,
 ):
     o = lax.axis_index("outer")
     i = lax.axis_index("inner")
@@ -155,40 +158,24 @@
     def gw_out(f):
         return pltpu.make_async_copy(gout.at[f], gw_hbm.at[:, f_cols(f)], sem_gw)
 
-    def red_c(n):
-        return remote(send_c.at[n], recv_c.at[n], c_s, c_r.at[n], dev_c)
-
-    def red_x(n, d):
-        return remote(send_x.at[n, d], recv_x.at[n, d], rx_s.at[d], rx_r.at[n], dev_x[d])
-
-    def red_up(n):
-        return remote(send_l.at[n], recv_l.at[n, 0], l_s, l_r.at[n, 0], at(h, y, (l + 1) % 4, x, c))
-
-    def red_down(n):
-        return remote(send_l.at[n], recv_l.at[n, 1], l_s, l_r.at[n, 1], at(h, y, (l + 3) % 4, x, c))
-
-    def red_far(n):
-        return remote(send_l.at[n], recv_f, l_s, lf_r, at(h, y, (l + 2) % 4, x, c))
-
-    def red_send(t):
-        far = (t // 2 == H - 1) & (((l == 3) & (root_l(t) == 1)) | ((l == 0) & (root_l(t) == 2)))
-
-        @pl.when((l > root_l(t)) & jnp.logical_not(far))
-        def _():
-            red_down(t // 2).start()
-
-        @pl.when((l < root_l(t)) & jnp.logical_not(far))
-        def _():
-            red_up(t // 2).start()
-
-        @pl.when(far)
-        def _():
-            red_far(t // 2).start()
+    def red_c(n, s):
+        return remote(send_c.at[n, :, HALVES[s]], recv_c.at[n, :, HALVES[s]], c_s, c_r.at[n, s], dev_c)
+
+    def red_x(n, d, s):
+        part = (n, d, slice(None), slice(None), HALVES[s])
+        return remote(send_x.at[part], recv_x.at[part], rx_s.at[d], rx_r.at[n, s], dev_x[d])
+
+    def red_l(n, s, away):
+        part = send_l.at[n, :, :, HALVES[s]]
+        return remote(
+            part, recv_l.at[away - 1, :, :, HALVES[s]], l_s, l_r.at[away - 1, s], at(h, y, (l + 4 - away) % 4, x, c)
+        )
 
     mine = h * 2 + pair
 
-    def final(n):
-        return remote(send_f.at[n], fin.at[mine], f_s, f_r, (dev_z, dev_d, dev_b)[n])
+    def final(n, s):
+        part = send_f.at[n, :, HALVES[s]]
+        return remote(part, fin.at[mine, :, HALVES[s]], f_s, f_r, (dev_z, dev_d, dev_b)[n])
 
     def ig_out(n):
         return pltpu.make_async_copy(fin.at[n], ig_hbm.at[:, n * DP : (n + 1) * DP], sem_ig)
@@ -264,9 +251,6 @@
         gout[f] = total.T
         gw_out(f).start()
 
-    def end(t):
-        return ((l == 0) & (root_l(t) > 0)) | ((l == 3) & (root_l(t) < 3)) | ((l != root_l(t)) & (t // 2 == H - 1))
-
     def step_body(step, carry):
         def s4(t, f, k):
             hid_b(k).wait_recv()
@@ -330,18 +314,20 @@
 
             @pl.when(c == root_c(t))
             def _():
-                red_c(n).wait_recv()
-                for d in (1, 2, 3, 0):
-                    xx = (x + d) % 4
-                    for block in range(4):
-                        rows = pl.ds(pl.multiple_of(block * TC + xx * 16, 16), 16)
-                        value = acc[n, rows, :] + recv_c[n, rows, :].astype(F32)
-                        if d == 0:
-                            keep_x[n, block] = value
-                        else:
-                            send_x[n, d - 1, block] = value.astype(BF16)
-                    if d:
-                        red_x(n, d - 1).start()
+                for s in range(2):
+                    cols = HALVES[s]
+                    red_c(n, s).wait_recv()
+                    for d in (1, 2, 3, 0):
+                        xx = (x + d) % 4
+                        for block in range(4):
+                            rows = pl.ds(pl.multiple_of(block * TC + xx * 16, 16), 16)
+                            value = acc[n, rows, cols] + recv_c[n, rows, cols].astype(F32)
+                            if d == 0:
+                                keep_x[n, block, :, cols] = value
+                            else:
+                                send_x[n, d - 1, block, :, cols] = value.astype(BF16)
+                        if d:
+                            red_x(n, d - 1, s).start()
 
         stage_t(step, O_R1, r1)
 
@@ -367,10 +353,11 @@
 
             @pl.when((f == F - 1) & (c != root_c(t)))
             def _():
-                for j in range(DP // COLS):
-                    cols = pl.ds(j * COLS, COLS)
-                    send_c[t // 2, :, cols] = partial(cols).astype(BF16)
-                red_c(t // 2).start()
+                for s in range(2):
+                    for j in range(DB // COLS):
+                        cols = pl.ds(s * DB + j * COLS, COLS)
+                        send_c[t // 2, :, cols] = partial(cols).astype(BF16)
+                    red_c(t // 2, s).start()
 
             for j in range(DP // COLS):
                 cols = pl.ds(j * COLS, COLS)
@@ -392,38 +379,23 @@
 
             @pl.when(c == root_c(t))
             def _():
-                remote(send_x.at[n], recv_x.at[n], rx_s.at[0], rx_r.at[n], dev_c).wait_recv()
-                value = keep_x[n]
-                for d in range(3):
-                    value = value + recv_x[n, d].astype(F32)
-
-                keep_x[n] = value
-
-                @pl.when(end(t))
-                def _():
-                    send_l[n] = value.astype(BF16)
-                    red_send(t)
+                for s in range(2):
+                    cols = HALVES[s]
+                    part = recv_x.at[n, :, :, :, cols]
+                    remote(part, part, rx_s.at[0], rx_r.at[n, s], dev_c).wait_recv()
+                    value = keep_x[n, :, :, cols]
+                    for d in range(3):
+                        value = value + recv_x[n, d, :, :, cols].astype(F32)
+                    keep_x[n, :, :, cols] = value
+                    send_l[n, :, :, cols] = value.astype(BF16)
+
+                    for away in (1, 2, 3):
+
+                        @pl.when((l - root_l(t) + 4) % 4 == away)
+                        def _(s=s, away=away):
+                            red_l(n, s, away).start()
 
         stage_t(step, O_R2, r2)
-
-        for depth in (1, 2):
-
-            def r3(t):
-                n = t // 2
-
-                @pl.when((c == root_c(t)) & (l < root_l(t)) & (l == depth) & (n < H - 1))
-                def _():
-                    red_up(n).wait_recv()
-                    send_l[n] = (keep_x[n] + recv_l[n, 0].astype(F32)).astype(BF16)
-                    red_up(n).start()
-
-                @pl.when((c == root_c(t)) & (l > root_l(t)) & (3 - l == depth) & (n < H - 1))
-                def _():
-                    red_down(n).wait_recv()
-                    send_l[n] = (keep_x[n] + recv_l[n, 1].astype(F32)).astype(BF16)
-                    red_down(n).start()
-
-            stage_t(step, O_R2 + O_R3 * depth, r3)
 
         return carry
 
@@ -434,27 +406,18 @@
 
     last = l // 3 + (l + 1) // 2 % 2 * (2 + (l + c + 1) % 2)
 
-    @pl.when(l > 0)
-    def _():
-        red_up(last).wait_recv()
-        keep_x[last] += recv_l[last, 0].astype(F32)
-
-    @pl.when(l < 3)
-    def _():
-        red_down(last).wait_recv()
-        keep_x[last] += recv_l[last, 1].astype(F32)
-
-    @pl.when(last == H - 1)
-    def _():
-        red_far(last).wait_recv()
-        keep_x[last] += recv_f[...].astype(F32)
-
-    value = keep_x[last]
-    value = value.astype(BF16)
-    fin[mine] = value[OWN]
-    for n in range(3):
-        send_f[n] = value[n + 1]
-        final(n).start()
+    for s in range(2):
+        cols = HALVES[s]
+
+        value = keep_x[last, :, :, cols]
+        for away in (1, 2, 3):
+            red_l(0, s, away).wait_recv()
+            value = value + recv_l[away - 1, :, :, cols].astype(F32)
+        value = value.astype(BF16)
+        fin[mine, :, cols] = value[OWN]
+        for n in range(3):
+            send_f[n, :, cols] = value[n + 1]
+            final(n, s).start()
 
     average(F - 1)
 
@@ -508,8 +471,7 @@
         pltpu.VMEM((H, 3, 4, 16, DP), BF16),
         pltpu.VMEM((H, 4, 16, DP), F32),
         pltpu.VMEM((H, 4, 16, DP), BF16),
-        pltpu.VMEM((H, 2, 4, 16, DP), BF16),
-        pltpu.VMEM((4, 16, DP), BF16),
+        pltpu.VMEM((3, 4, 16, DP), BF16),
         pltpu.VMEM((3, 16, DP), BF16),
         pltpu.VMEM((4, 16, DP), BF16),
         pltpu.VMEM((F, FC, DB), BF16),
@@ -518,7 +480,7 @@
         dma, dma((3,)), dma, dma,
         dma, dma, dma, dma((T,)), dma((3,)), dma((T,)), dma, dma((T,)),
         dma, dma((F,)), dma, dma((K,)), dma, dma((K,)), dma, dma((K,)), dma, dma, dma((K,)),
-        dma, dma((F,)), dma, dma((H,)), dma((3,)), dma((H,)), dma, dma((H, 2)), dma, dma, dma,
+        dma, dma((F,)), dma, dma((H, 2)), dma((3,)), dma((H, 2)), dma, dma((3, 2)), dma, dma,
     ]
 
 

time: 143 us -> 141 us (0.986)
  the two profiles are of different devices: /device:TPU:88 before, /device:TPU:32 now
where the time goes in v5:
time: 141 us; the launch traced here: 139 us
  Pallas kernels  134 us (95%)
  other arithmetic  3.26 us (2%)
    pallas_call x1, Pallas kernels, local(): pl.pallas_call(kernel, out_shape=(jax.ShapeDtypeStruct((16, 6144), BF16),...  134 us
    mul x1, other arithmetic, local(): return (input_grad, in_grad * 0.125)  3.26 us

profile of v5, /device:TPU:32, one launch (start us, length us, event | category | flops | bytes accessed | tf_op | source)
XLA Modules:
  0.0 138.5 jit_solution(10352355815067746640)
XLA Ops:
  0.6 134.0 %ffn_in_backward.1 = (bf16[16,6144]{1,0:T(8,128)(2,1)}, f32[768,768]{1,0:T(8,128)}) custom-call(bf16[4,4,2,16,6144]{4,3,2,1,0:T(8,128)(2,1)} %bitcast.2, bf16[4,4,2,16,768]{4,3,2,1,0:T(8,128)(2,1)} %bitcast.3, bf16[768,768]{1,0:T(8,128)(2,1)} %codes_hbm.1, bf16[768]{0:T(1024)(128)(2,1)} %scales_hbm.1), custom_call_target="tpu_custom_call" | custom-call | flops 14495514624 | bytes 12582912 | tf_op jit(solution)/shard_map/ffn_in_backward/pallas_call | solution.py:488
  134.6 0.0 copy-start
  134.6 3.3 %broadcast_multiply_fusion = f32[768,768]{1,0:T(8,128)} fusion(f32[768,768]{1,0:T(8,128)} %get-tuple-element.5), kind=kLoop, calls=%fused_computation | loop fusion | flops 589824 | bytes 4718592 | tf_op jit(solution)/shard_map/mul | solution.py:513
  137.9 0.0 copy-done
  137.9 0.7 copy.7
Async XLA Ops:
  134.6 3.3 %copy-start = (bf16[16,6144]{1,0:T(8,128)(2,1)S(1)}, bf16[16,6144]{1,0:T(8,128)(2,1)}, u32[]{:S(2)}) copy-start(bf16[16,6144]{1,0:T(8,128)(2,1)} %get-tuple-element.8) | copy-start | bytes 589828

commit v6 on v5

--- a/solution.py
+++ b/solution.py
@@ -321,7 +321,7 @@
                         xx = (x + d) % 4
                         for block in range(4):
                             rows = pl.ds(pl.multiple_of(block * TC + xx * 16, 16), 16)
-                            value = acc[n, rows, cols] + recv_c[n, rows, cols].astype(F32)
+                            value = acc[t, rows, cols] + recv_c[n, rows, cols].astype(F32)
                             if d == 0:
                                 keep_x[n, block, :, cols] = value
                             else:
@@ -337,26 +337,28 @@
             grads = hg[k].reshape(4 * TC, FC)
 
             def partial(cols):
-                return sum(
-                    lax.dot_general(
-                        hg[t * F + n].reshape(4 * TC, FC), ws[n, cols, :],
-                        (((1,), (1,)), ((), ())), preferred_element_type=F32,
-                    )
-                    for n in range(F)
+                return lax.dot_general(
+                    grads, ws[f, cols, :], (((1,), (1,)), ((), ())), preferred_element_type=F32
                 )
 
-            @pl.when((f == F - 1) & (c == root_c(t)))
+            @pl.when(f == 0)
             def _():
                 for j in range(DP // COLS):
                     cols = pl.ds(j * COLS, COLS)
-                    acc[t // 2, :, cols] = partial(cols)
+                    acc[t, :, cols] = partial(cols)
+
+            @pl.when((f > 0) & ((f < F - 1) | (c == root_c(t))))
+            def _():
+                for j in range(DP // COLS):
+                    cols = pl.ds(j * COLS, COLS)
+                    acc[t, :, cols] += partial(cols)
 
             @pl.when((f == F - 1) & (c != root_c(t)))
             def _():
                 for s in range(2):
                     for j in range(DB // COLS):
                         cols = pl.ds(s * DB + j * COLS, COLS)
-                        send_c[t // 2, :, cols] = partial(cols).astype(BF16)
+                        send_c[t // 2, :, cols] = (acc[t, :, cols] + partial(cols)).astype(BF16)
                     red_c(t // 2, s).start()
 
             for j in range(DP // COLS):
@@ -464,7 +466,7 @@
         pltpu.VMEM((K, TC, FC), BF16),
         pltpu.VMEM((K, 4, TC, FC), BF16),
         pltpu.VMEM((F, FC, DP), F32),
-        pltpu.VMEM((H, 4 * TC, DP), F32),
+        pltpu.VMEM((T, 4 * TC, DP), F32),
         pltpu.VMEM((H, 4 * TC, DP), BF16),
         pltpu.VMEM((H, 4 * TC, DP), BF16),
         pltpu.VMEM((H, 3, 4, 16, DP), BF16),

time: 141 us -> 143 us (1.014)
  the two profiles are of different devices: /device:TPU:32 before, /device:TPU:36 now
where the time goes in v6:
time: 143 us
  Pallas kernels  138 us (97%)
  other arithmetic  3.26 us (2%)
    pallas_call x1, Pallas kernels, local(): pl.pallas_call(kernel, out_shape=(jax.ShapeDtypeStruct((16, 6144), BF16),...  138 us
    mul x1, other arithmetic, local(): return (input_grad, in_grad * 0.125)  3.26 us

profile of v6, /device:TPU:36, one launch (start us, length us, event | category | flops | bytes accessed | tf_op | source)
XLA Modules:
  0.0 143.0 jit_solution(8983919826067860350)
XLA Ops:
  0.6 138.4 %ffn_in_backward.1 = (bf16[16,6144]{1,0:T(8,128)(2,1)}, f32[768,768]{1,0:T(8,128)}) custom-call(bf16[4,4,2,16,6144]{4,3,2,1,0:T(8,128)(2,1)} %bitcast.2, bf16[4,4,2,16,768]{4,3,2,1,0:T(8,128)(2,1)} %bitcast.3, bf16[768,768]{1,0:T(8,128)(2,1)} %codes_hbm.1, bf16[768]{0:T(1024)(128)(2,1)} %scales_hbm.1), custom_call_target="tpu_custom_call" | custom-call | flops 14495514624 | bytes 12582912 | tf_op jit(solution)/shard_map/ffn_in_backward/pallas_call | solution.py:490
  139.0 0.0 copy-start
  139.0 3.3 %broadcast_multiply_fusion = f32[768,768]{1,0:T(8,128)} fusion(f32[768,768]{1,0:T(8,128)} %get-tuple-element.5), kind=kLoop, calls=%fused_computation | loop fusion | flops 589824 | bytes 4718592 | tf_op jit(solution)/shard_map/mul | solution.py:515
  142.3 0.0 copy-done
  142.3 0.7 copy.7
Async XLA Ops:
  139.0 3.3 %copy-start = (bf16[16,6144]{1,0:T(8,128)(2,1)S(1)}, bf16[16,6144]{1,0:T(8,128)(2,1)}, u32[]{:S(2)}) copy-start(bf16[16,6144]{1,0:T(8,128)(2,1)} %get-tuple-element.8) | copy-start | bytes 589828

commit v7 on v5

--- a/solution.py
+++ b/solution.py
@@ -198,7 +198,7 @@
     def x_share(t):
         part = xs.at[t, 1:4, x, :, half]
         remote(part, part, xc_s, xp_r.at[t], dev_c).wait_recv()
-        for d in range(3):
+        for d in (1, 0, 2):
             x_x(t, d).start()
 
     def x_core(t):
@@ -317,7 +317,7 @@
                 for s in range(2):
                     cols = HALVES[s]
                     red_c(n, s).wait_recv()
-                    for d in (1, 2, 3, 0):
+                    for d in (2, 1, 3, 0):
                         xx = (x + d) % 4
                         for block in range(4):
                             rows = pl.ds(pl.multiple_of(block * TC + xx * 16, 16), 16)
@@ -415,7 +415,7 @@
             value = value + recv_l[away - 1, :, :, cols].astype(F32)
         value = value.astype(BF16)
         fin[mine, :, cols] = value[OWN]
-        for n in range(3):
+        for n in (1, 0, 2):
             send_f[n, :, cols] = value[n + 1]
             final(n, s).start()
 

time: 141 us -> 140 us (level); the launches traced: 139 us -> 139 us
  no operation moved by 1% of the time
where the time goes in v7:
time: 140 us; the launch traced here: 139 us
  Pallas kernels  135 us (96%)
  other arithmetic  3.26 us (2%)
    pallas_call x1, Pallas kernels, local(): pl.pallas_call(kernel, out_shape=(jax.ShapeDtypeStruct((16, 6144), BF16),...  135 us
    mul x1, other arithmetic, local(): return (input_grad, in_grad * 0.125)  3.26 us

profile of v7, /device:TPU:32, one launch (start us, length us, event | category | flops | bytes accessed | tf_op | source)
XLA Modules:
  0.0 139.4 jit_solution(1672798085020919926)
XLA Ops:
  0.6 134.8 %ffn_in_backward.1 = (bf16[16,6144]{1,0:T(8,128)(2,1)}, f32[768,768]{1,0:T(8,128)}) custom-call(bf16[4,4,2,16,6144]{4,3,2,1,0:T(8,128)(2,1)} %bitcast.2, bf16[4,4,2,16,768]{4,3,2,1,0:T(8,128)(2,1)} %bitcast.3, bf16[768,768]{1,0:T(8,128)(2,1)} %codes_hbm.1, bf16[768]{0:T(1024)(128)(2,1)} %scales_hbm.1), custom_call_target="tpu_custom_call" | custom-call | flops 14495514624 | bytes 12582912 | tf_op jit(solution)/shard_map/ffn_in_backward/pallas_call | solution.py:488
  135.4 0.0 copy-start
  135.4 3.3 %broadcast_multiply_fusion = f32[768,768]{1,0:T(8,128)} fusion(f32[768,768]{1,0:T(8,128)} %get-tuple-element.5), kind=kLoop, calls=%fused_computation | loop fusion | flops 589824 | bytes 4718592 | tf_op jit(solution)/shard_map/mul | solution.py:513
  138.7 0.0 copy-done
  138.7 0.7 copy.7
Async XLA Ops:
  135.4 3.3 %copy-start = (bf16[16,6144]{1,0:T(8,128)(2,1)S(1)}, bf16[16,6144]{1,0:T(8,128)(2,1)}, u32[]{:S(2)}) copy-start(bf16[16,6144]{1,0:T(8,128)(2,1)} %get-tuple-element.8) | copy-start | bytes 589828
